TPU v7x, 32 devices: a whole 2x2x4 slice. The times are simulated.
32 devices in a mesh: tm: 8 (over z, y), head: 4 (over x, core).
Axes of the slice: x: 2, y: 2, z: 4, core: 2. Of those that a mesh axis runs over, the one named last changes fastest.
Arguments:
- feats_long: bfloat16 [8192, 80], P(('tm', 'head')), may hold values from -6 to 6
- feats_short: bfloat16 [49152, 80], P(('tm', 'head')), may hold values from -6 to 6
- long_length: int32 [1], replicated, may hold values from 1985 to 2048
- short_groups: int32 [32, 4], P(('tm', 'head')), may hold values from 1 to 6, 12 in all within a row
- freq_start: int32 [32], P(('tm', 'head')), may hold values from 0 to 53
- freq_width: int32 [32], P(('tm', 'head')), may hold values from 0 to 27
- time_start: int32 [32], P(('tm', 'head')), may hold values from 0 to 1436
- time_width: int32 [32], P(('tm', 'head')), may hold values from 0 to 100
- stem_weight: bfloat16 [512, 320], P(('tm', 'head')), may hold values from -0.3125 to 0.3125
- norm_gains: bfloat16 [512, 6], P(('tm', 'head')), may hold values from 0.25 to 1.75
- ffn1_up: bfloat16 [512, 2048], P(('tm', 'head')), may hold values from -0.25 to 0.25
- ffn1_down: bfloat16 [2048, 512], P(('tm', 'head')), may hold values from -0.125 to 0.125
- mixer_in: bfloat16 [512, 1024], P(('tm', 'head')), may hold values from -0.25 to 0.25
- mixer_out: bfloat16 [512, 512], P(('tm', 'head')), may hold values from -0.25 to 0.25
- mixer_log_rate: bfloat16 [512, 32], P(('tm', 'head')), may hold values from -12 to -2
- mixer_freq: bfloat16 [512, 32], P(('tm', 'head')), may hold values from -3.140625 to 3.140625
- mixer_coef: bfloat16 [512, 64], P(('tm', 'head')), may hold values from -1 to 1
- conv_taps: bfloat16 [512, 15], P(('tm', 'head')), may hold values from -1.5 to 1.5
- ffn2_up: bfloat16 [512, 2048], P(('tm', 'head')), may hold values from -0.25 to 0.25
- ffn2_down: bfloat16 [2048, 512], P(('tm', 'head')), may hold values from -0.125 to 0.125
- cotangent_long: bfloat16 [2048, 512], P(('tm', 'head')), may hold values from -6 to 6
- cotangent_short: bfloat16 [12288, 512], P(('tm', 'head')), may hold values from -6 to 6
Outputs:
- output_long: bfloat16 [2048, 512], P(('tm', 'head'))
- output_short: bfloat16 [12288, 512], P(('tm', 'head'))
- grad_feats_long: bfloat16 [8192, 80], P(('tm', 'head'))
- grad_feats_short: bfloat16 [49152, 80], P(('tm', 'head'))
- grad_stem_weight: float32 [512, 320], P(('tm', 'head'))
- grad_norm_gains: float32 [512, 6], P(('tm', 'head'))
- grad_ffn1_up: float32 [512, 2048], P(('tm', 'head'))
- grad_ffn1_down: float32 [2048, 512], P(('tm', 'head'))
- grad_mixer_in: float32 [512, 1024], P(('tm', 'head'))
- grad_mixer_out: float32 [512, 512], P(('tm', 'head'))
- grad_mixer_log_rate: float32 [512, 32], P(('tm', 'head'))
- grad_mixer_freq: float32 [512, 32], P(('tm', 'head'))
- grad_mixer_coef: float32 [512, 64], P(('tm', 'head'))
- grad_conv_taps: float32 [512, 15], P(('tm', 'head'))
- grad_ffn2_up: float32 [512, 2048], P(('tm', 'head'))
- grad_ffn2_down: float32 [2048, 512], P(('tm', 'head'))
Inputs may be any that keep to these rules, and one draw needn't show every extreme that they name: `short_groups`: each row lists, in blocks of 32 frames, the lengths of the utterances that fill one device's 384 short frames in order; a row sums to 12.
All inputs are finite; a program needn't handle non-finite values.
Results may differ from a plain program's by a relative error of at most 0.018.
Values may be sent and summed in bfloat16 or wider, within the bound.
No kernel may reach another device: no remote copies, remote signals or barrier semaphores. Data moves between devices by JAX's collectives and lax.ppermute only.
A program may use at most 384 MiB of HBM per device.

v0:
```python
from functools import partial

import jax
import jax.numpy as jnp
from jax import lax
from jax.sharding import PartitionSpec as P

GROUP = 32


highest = lax.Precision.HIGHEST


def prefix_2(x, axis, join, neutral):
    place = lax.axis_index(axis)
    gathered = jax.tree.map(
        lambda a, kind: lax.all_gather(a.astype(kind), axis),
        x,
        (jnp.bfloat16, jnp.bfloat16, jnp.bfloat16, jnp.bfloat16),
    )
    state = jax.tree.map(lambda a, e: jnp.zeros_like(a) + jnp.asarray(e, a.dtype), x, neutral)

    def one(hop, state):
        return join(
            state,
            jax.tree.map(
                lambda a, own: lax.dynamic_index_in_dim(a, hop, 0, False).astype(own.dtype),
                gathered,
                x,
            ),
        )

    return lax.fori_loop(0, place, one, state)


def prefix_3(x, axis, join, neutral):
    count = lax.axis_size(axis)
    place = lax.axis_index(axis)
    ahead = count - 1 - place
    gathered = jax.tree.map(
        lambda a, kind: lax.all_gather(a.astype(kind), axis),
        x,
        jax.tree.map(lambda a: jnp.bfloat16 if a.dtype == jnp.float32 else a.dtype, x),
    )
    state = jax.tree.map(lambda a, e: jnp.zeros_like(a) + jnp.asarray(e, a.dtype), x, neutral)

    def one(hop, state):
        source = count - 1 - hop
        return join(
            state,
            jax.tree.map(
                lambda a, own: lax.dynamic_index_in_dim(a, source, 0, False).astype(own.dtype),
                gathered,
                x,
            ),
        )

    return lax.fori_loop(0, ahead, one, state)


def extended(x, sides, width):
    for axis, dim in sides:
        size, length = (lax.axis_size(axis), x.shape[dim])
        up = [(i, (i + 1) % size) for i in range(size - 1)]
        down = [(j, i) for i, j in up]
        last = lax.slice_in_dim(x, length - width, length, axis=dim)
        leading = lax.slice_in_dim(x, 0, width, axis=dim)
        before = lax.ppermute(last, axis, up)
        after = lax.ppermute(leading, axis, down)
        x = jnp.concatenate([before, x, after], axis=dim)
    return x


def norm_rows(values, gain_row):
    centred = values - jnp.mean(values, axis=-1, keepdims=True)
    variance = jnp.mean(centred * centred, axis=-1, keepdims=True)
    return centred * lax.rsqrt(variance + 1e-05) * gain_row


def ssm_tables(log_rate, freq_values, coef_values, block_width):
    rate_values = jnp.exp(log_rate)
    step_index = jnp.arange(block_width + 1).astype(jnp.float32)
    decays = jnp.exp(-rate_values[:, :, None] * step_index)
    phases = freq_values[:, :, None] * step_index
    scales = jnp.sqrt(2.0 * rate_values)
    states = log_rate.shape[1]
    return (
        decays * jnp.cos(phases),
        decays * jnp.sin(phases),
        scales * coef_values[:, :states],
        scales * coef_values[:, states:],
    )


def chain_step(previous, current):
    return (
        current[0] * previous[0] - current[1] * previous[1],
        current[0] * previous[1] + current[1] * previous[0],
        current[0] * previous[2] - current[1] * previous[3] + current[2],
        current[0] * previous[3] + current[1] * previous[2] + current[3],
    )


def group_scan(source, keep_flags, tables, start_real, start_imaginary):
    power_real, power_imaginary, weight_real, weight_imaginary = tables
    block_width = power_real.shape[2] - 1
    row_count, channels = source.shape
    block_count = row_count // block_width
    kernel = jnp.sum(
        weight_real[:, :, None] * power_real[:, :, :block_width]
        - weight_imaginary[:, :, None] * power_imaginary[:, :, :block_width],
        axis=1,
    )
    lag_index = jnp.arange(block_width)[:, None] - jnp.arange(block_width)[None, :]
    toeplitz = jnp.where(
        lag_index[None] >= 0, kernel[:, jnp.clip(lag_index, 0, block_width - 1)], 0.0
    )
    blocks = source.reshape(block_count, block_width, channels)
    within = jnp.einsum("cts,jsc->jtc", toeplitz, blocks, precision=highest)
    flip_real = power_real[:, :, :block_width][:, :, ::-1]
    flip_imaginary = power_imaginary[:, :, :block_width][:, :, ::-1]
    added_real = jnp.einsum("jsc,cns->jcn", blocks, flip_real, precision=highest)
    added_imaginary = jnp.einsum("jsc,cns->jcn", blocks, flip_imaginary, precision=highest)
    scale_real = keep_flags[:, None, None] * power_real[None, :, :, block_width]
    scale_imaginary = keep_flags[:, None, None] * power_imaginary[None, :, :, block_width]
    totals = lax.associative_scan(
        chain_step, (scale_real, scale_imaginary, added_real, added_imaginary), axis=0
    )
    state_real = totals[2] + totals[0] * start_real - totals[1] * start_imaginary
    state_imaginary = totals[3] + totals[0] * start_imaginary + totals[1] * start_real
    before_real = jnp.concatenate([start_real[None], state_real[:-1]], axis=0)
    before_imaginary = jnp.concatenate([start_imaginary[None], state_imaginary[:-1]], axis=0)
    lead_real = (
        weight_real[:, :, None] * power_real[:, :, 1:]
        - weight_imaginary[:, :, None] * power_imaginary[:, :, 1:]
    )
    lead_imaginary = (
        weight_real[:, :, None] * power_imaginary[:, :, 1:]
        + weight_imaginary[:, :, None] * power_real[:, :, 1:]
    )
    carried = jnp.einsum("jcn,cnt->jtc", before_real, lead_real, precision=highest) - jnp.einsum(
        "jcn,cnt->jtc", before_imaginary, lead_imaginary, precision=highest
    )
    mixed_out = within + carried * keep_flags[:, None, None]
    return (mixed_out.reshape(row_count, channels), state_real[-1], state_imaginary[-1])


def group_keep(utter_ids, block_width):
    firsts = utter_ids[::block_width]
    last_ids = jnp.concatenate(
        [jnp.full((1,), -1, jnp.int32), utter_ids[block_width - 1 :: block_width][:-1]]
    )
    return (firsts == last_ids).astype(jnp.float32)


def rim_mask(utter_ids, half_span):
    row_count = utter_ids.shape[0]
    padded = jnp.pad(utter_ids, (half_span, half_span), constant_values=-1)
    return jnp.stack(
        [
            (padded[offset : offset + row_count] == utter_ids).astype(jnp.float32)
            for offset in range(2 * half_span + 1)
        ],
        axis=1,
    )


def depthwise(padded, same_mask, conv_taps):
    row_count = same_mask.shape[0]
    summed = jnp.zeros((row_count, padded.shape[1]), jnp.float32)
    for offset in range(conv_taps.shape[1]):
        summed = (
            summed
            + padded[offset : offset + row_count]
            * same_mask[:, offset : offset + 1]
            * conv_taps[:, offset]
        )
    return summed


def silu_slope(values):
    logistic = jax.nn.sigmoid(values)
    return logistic * (1.0 + values * (1.0 - logistic))


def row_dot(first_op, second_op):
    return jnp.dot(first_op, second_op, preferred_element_type=jnp.float32)


def inner_dot(first_op, second_op):
    return lax.dot_general(
        first_op, second_op, (((0,), (0,)), ((), ())), preferred_element_type=jnp.float32
    )


def outer_dot(first_op, second_op):
    return lax.dot_general(
        first_op, second_op, (((1,), (1,)), ((), ())), preferred_element_type=jnp.float32
    )


def ffn_forward(residual, gain_row, weight_up, weight_down):
    normed, norm_back = jax.vjp(norm_rows, residual, gain_row)
    normed_b = normed.astype(jnp.bfloat16)
    hidden = row_dot(normed_b, weight_up)
    active = jax.nn.silu(hidden).astype(jnp.bfloat16)
    return (row_dot(active, weight_down), (normed_b, hidden, active, norm_back))


def ffn_backward(grad_out, kept_state, weight_up, weight_down):
    normed_b, hidden, active, norm_back = kept_state
    grad_b = grad_out.astype(jnp.bfloat16)
    grad_down = inner_dot(active, grad_b)
    grad_active = outer_dot(grad_b, weight_down)
    grad_hidden = (grad_active * silu_slope(hidden)).astype(jnp.bfloat16)
    grad_up = inner_dot(normed_b, grad_hidden)
    grad_residual, grad_gain = norm_back(outer_dot(grad_hidden, weight_up))
    return (grad_residual, grad_gain, grad_up, grad_down)


def long_local(source, log_rate, freq_values, coef_values):
    tables = ssm_tables(log_rate, freq_values, coef_values, GROUP)
    row_count = source.shape[0]
    zero_state = jnp.zeros(log_rate.shape, jnp.float32)
    keep_flags = jnp.ones((row_count // GROUP,), jnp.float32)
    mixed_out, end_real, end_imaginary = group_scan(
        source, keep_flags, tables, zero_state, zero_state
    )
    decays = jnp.exp(-jnp.exp(log_rate) * row_count)
    return (
        mixed_out,
        end_real,
        end_imaginary,
        decays * jnp.cos(freq_values * row_count),
        decays * jnp.sin(freq_values * row_count),
    )


def long_carry(start_real, start_imaginary, log_rate, freq_values, coef_values, row_count):
    power_real, power_imaginary, weight_real, weight_imaginary = ssm_tables(
        log_rate, freq_values, coef_values, row_count
    )
    lead_real = (
        weight_real[:, :, None] * power_real[:, :, 1:]
        - weight_imaginary[:, :, None] * power_imaginary[:, :, 1:]
    )
    lead_imaginary = (
        weight_real[:, :, None] * power_imaginary[:, :, 1:]
        + weight_imaginary[:, :, None] * power_real[:, :, 1:]
    )
    return jnp.einsum("cnr,cn->rc", lead_real, start_real, precision=highest) - jnp.einsum(
        "cnr,cn->rc", lead_imaginary, start_imaginary, precision=highest
    )


def local(
    feats_long,
    feats_short,
    long_length,
    short_groups,
    freq_start,
    freq_width,
    time_start,
    time_width,
    stem_weight,
    norm_gains,
    ffn1_up,
    ffn1_down,
    mixer_in,
    mixer_out,
    mixer_log_rate,
    mixer_freq,
    mixer_coef,
    conv_taps,
    ffn2_up,
    ffn2_down,
    cotangent_long,
    cotangent_short,
):
    params = (
        lax.all_gather(stem_weight, ("tm", "head"), axis=0, tiled=True),
        lax.all_gather(norm_gains, ("tm", "head"), axis=0, tiled=True),
        lax.all_gather(ffn1_up, ("tm", "head"), axis=0, tiled=True),
        lax.all_gather(ffn1_down, ("tm", "head"), axis=0, tiled=True),
        lax.all_gather(mixer_in, ("tm", "head"), axis=0, tiled=True),
        lax.all_gather(mixer_out, ("tm", "head"), axis=0, tiled=True),
        lax.all_gather(mixer_log_rate, ("tm", "head"), axis=0, tiled=True),
        lax.all_gather(mixer_freq, ("tm", "head"), axis=0, tiled=True),
        lax.all_gather(mixer_coef, ("tm", "head"), axis=0, tiled=True),
        lax.all_gather(conv_taps, ("tm", "head"), axis=0, tiled=True),
        lax.all_gather(ffn2_up, ("tm", "head"), axis=0, tiled=True),
        lax.all_gather(ffn2_down, ("tm", "head"), axis=0, tiled=True),
    )
    (
        stem_full,
        gains_full,
        up_first,
        down_first,
        proj_in,
        proj_out,
        rate_full,
        freq_full,
        coef_full,
        taps_full,
        up_second,
        down_second,
    ) = params
    gain_values = gains_full.astype(jnp.float32)
    log_rate = rate_full.astype(jnp.float32)
    freq_values = freq_full.astype(jnp.float32)
    coef_values = coef_full.astype(jnp.float32)
    taps_values = taps_full.astype(jnp.float32)
    features = gains_full.shape[0]
    long_rows = feats_long.shape[0] // 4
    short_rows = feats_short.shape[0] // 4
    mel_bins = feats_long.shape[1]
    mel_index = jnp.arange(mel_bins)
    mel_band = (mel_index >= freq_start[0]) & (mel_index < freq_start[0] + freq_width[0])
    freq_keep = (1 - mel_band.astype(jnp.int32)).astype(jnp.bfloat16)
    row_index = jnp.arange(4 * short_rows)
    time_blank = (row_index >= time_start[0]) & (row_index < time_start[0] + time_width[0])
    time_keep = (1 - time_blank.astype(jnp.int32)).astype(jnp.bfloat16)
    stacked = jnp.concatenate(
        [
            (feats_long * freq_keep[None, :]).reshape(long_rows, 4 * mel_bins),
            (feats_short * freq_keep[None, :] * time_keep[:, None]).reshape(
                short_rows, 4 * mel_bins
            ),
        ],
        axis=0,
    )
    position = lax.axis_index(("tm", "head")) * long_rows + jnp.arange(long_rows)
    valid_long = (position < long_length[0]).astype(jnp.float32)
    valid_rows = jnp.concatenate([valid_long, jnp.ones((short_rows,), jnp.float32)])
    valid_b = valid_rows.astype(jnp.bfloat16)[:, None]
    starts = jnp.cumsum(short_groups[0]) - short_groups[0]
    group_of = jnp.arange(short_rows) // GROUP
    short_ids = jnp.sum((starts[None, :] <= group_of[:, None]).astype(jnp.int32), axis=1) - 1
    residual = outer_dot(stacked, stem_full)
    ffn_first, kept_first = ffn_forward(residual, gain_values[:, 0], up_first, down_first)
    residual1 = residual + 0.5 * ffn_first
    normed2, norm2_back = jax.vjp(norm_rows, residual1, gain_values[:, 1])
    normed2_b = normed2.astype(jnp.bfloat16)
    projected = row_dot(normed2_b, proj_in)
    inputs_b = projected[:, :features].astype(jnp.bfloat16)
    gates = projected[:, features:]
    source_b = inputs_b * valid_b
    channels = features // lax.axis_size("head")
    offset = lax.axis_index("head") * channels
    rate_part = lax.dynamic_slice_in_dim(log_rate, offset, channels, 0)
    freq_part = lax.dynamic_slice_in_dim(freq_values, offset, channels, 0)
    coef_part = lax.dynamic_slice_in_dim(coef_values, offset, channels, 0)
    mixer_inputs = lax.all_to_all(
        source_b[:long_rows], "head", split_axis=1, concat_axis=0, tiled=True
    ).astype(jnp.float32)
    mixer_rows = mixer_inputs.shape[0]
    long_out, long_back = jax.vjp(long_local, mixer_inputs, rate_part, freq_part, coef_part)
    mixed_zero, end_real, end_imaginary, step_real, step_imaginary = long_out
    unit_state = (
        jnp.ones_like(step_real),
        jnp.zeros_like(step_real),
        jnp.zeros_like(step_real),
        jnp.zeros_like(step_real),
    )
    prefix = prefix_2(
        (step_real, step_imaginary, end_real, end_imaginary), "tm", chain_step, unit_state
    )
    start_real, start_imaginary = (prefix[2], prefix[3])
    carry_out, carry_back = jax.vjp(
        partial(long_carry, row_count=mixer_rows),
        start_real,
        start_imaginary,
        rate_part,
        freq_part,
        coef_part,
    )
    mixed_long = lax.all_to_all(
        (mixed_zero + carry_out).astype(jnp.bfloat16),
        "head",
        split_axis=0,
        concat_axis=1,
        tiled=True,
    )
    short_flags = group_keep(short_ids, GROUP)
    zero_state = jnp.zeros(log_rate.shape, jnp.float32)

    def short_mix(source, rate_values, freq_inputs, coef_inputs):
        return group_scan(
            source,
            short_flags,
            ssm_tables(rate_values, freq_inputs, coef_inputs, GROUP),
            zero_state,
            zero_state,
        )[0]

    mixed_short, short_back = jax.vjp(
        short_mix, source_b[long_rows:].astype(jnp.float32), log_rate, freq_values, coef_values
    )
    mixed_b = jnp.concatenate([mixed_long, mixed_short.astype(jnp.bfloat16)], axis=0)
    inputs_f = inputs_b.astype(jnp.float32)
    joined = mixed_b.astype(jnp.float32) + gain_values[:, 5] * inputs_f
    gate_act = jax.nn.silu(gates)
    gated_b = (joined * gate_act).astype(jnp.bfloat16)
    residual2 = residual1 + row_dot(gated_b, proj_out)
    normed3, norm3_back = jax.vjp(norm_rows, residual2, gain_values[:, 2])
    spread_b = normed3.astype(jnp.bfloat16) * valid_b
    half_span = taps_full.shape[1] // 2
    rim_long = extended(spread_b[:long_rows], ((("tm", "head"), 0),), half_span)
    rim_values = rim_long.astype(jnp.float32)
    pre_long = depthwise(
        rim_values, jnp.ones((long_rows, 2 * half_span + 1), jnp.float32), taps_values
    )
    short_same = rim_mask(short_ids, half_span)

    def short_conv(spread, taps_inputs):
        return depthwise(jnp.pad(spread, ((half_span, half_span), (0, 0))), short_same, taps_inputs)

    pre_short, conv_back = jax.vjp(
        short_conv, spread_b[long_rows:].astype(jnp.float32), taps_values
    )
    pre_conv = jnp.concatenate([pre_long, pre_short], axis=0)
    residual3 = residual2 + jax.nn.silu(pre_conv)
    ffn_second, kept_second = ffn_forward(residual3, gain_values[:, 3], up_second, down_second)
    residual4 = residual3 + 0.5 * ffn_second
    final_out, final_back = jax.vjp(norm_rows, residual4, gain_values[:, 4])
    out_long = final_out[:long_rows].astype(jnp.bfloat16)
    out_short = final_out[long_rows:].astype(jnp.bfloat16)
    cotangent = jnp.concatenate([cotangent_long, cotangent_short], axis=0).astype(jnp.float32)
    grad4, grad_gain_final = final_back(cotangent)
    piece_grad, grad_gain4, grad_up2, grad_down2 = ffn_backward(
        0.5 * grad4, kept_second, up_second, down_second
    )
    grad3 = grad4 + piece_grad
    grad_pre_b = (grad3 * silu_slope(pre_conv)).astype(jnp.bfloat16)
    grad_rim = extended(grad_pre_b[:long_rows], ((("tm", "head"), 0),), half_span).astype(
        jnp.float32
    )
    grad_spread_long = jnp.zeros((long_rows, features), jnp.float32)
    for tap_index in range(2 * half_span + 1):
        lead_row = 2 * half_span - tap_index
        grad_spread_long = (
            grad_spread_long + grad_rim[lead_row : lead_row + long_rows] * taps_values[:, tap_index]
        )
    grad_pre_long = grad_pre_b[:long_rows].astype(jnp.float32)
    grad_taps_long = jnp.stack(
        [
            jnp.sum(grad_pre_long * rim_values[tap_index : tap_index + long_rows], axis=0)
            for tap_index in range(2 * half_span + 1)
        ],
        axis=1,
    )
    grad_spread_short, grad_taps_short = conv_back(grad_pre_b[long_rows:].astype(jnp.float32))
    grad_normed3 = (
        jnp.concatenate([grad_spread_long, grad_spread_short], axis=0) * valid_rows[:, None]
    )
    piece_grad, grad_gain3 = norm3_back(grad_normed3)
    grad2 = grad3 + piece_grad
    grad_out_b = grad2.astype(jnp.bfloat16)
    grad_proj_out = inner_dot(gated_b, grad_out_b)
    grad_gated = outer_dot(grad_out_b, proj_out)
    grad_joined = grad_gated * gate_act
    grad_gates = grad_gated * joined * silu_slope(gates)
    grad_skip = jnp.sum(grad_joined * inputs_f, axis=0)
    grad_mixed_b = grad_joined.astype(jnp.bfloat16)
    grad_here = lax.all_to_all(
        grad_mixed_b[:long_rows], "head", split_axis=1, concat_axis=0, tiled=True
    ).astype(jnp.float32)
    grad_start_real, grad_start_imaginary, grad_rate_carry, grad_freq_carry, grad_coef_carry = (
        carry_back(grad_here)
    )
    suffix = prefix_3(
        (step_real, -step_imaginary, grad_start_real, grad_start_imaginary),
        "tm",
        chain_step,
        unit_state,
    )
    later_real, later_imaginary = (suffix[2], suffix[3])
    cross_real = later_real * start_real + later_imaginary * start_imaginary
    cross_imaginary = later_imaginary * start_real - later_real * start_imaginary
    grad_mixer_rows, grad_rate_long, grad_freq_long, grad_coef_long = long_back(
        (grad_here, later_real, later_imaginary, cross_real, cross_imaginary)
    )
    grad_source_long = lax.all_to_all(
        grad_mixer_rows.astype(jnp.bfloat16), "head", split_axis=0, concat_axis=1, tiled=True
    )
    grad_source_short, grad_rate_short, grad_freq_short, grad_coef_short = short_back(
        grad_mixed_b[long_rows:].astype(jnp.float32)
    )
    grad_source = jnp.concatenate(
        [grad_source_long, grad_source_short.astype(jnp.bfloat16)], axis=0
    ).astype(jnp.float32)
    grad_inputs = grad_source * valid_rows[:, None] + gain_values[:, 5] * grad_joined
    grad_proj_b = jnp.concatenate([grad_inputs, grad_gates], axis=1).astype(jnp.bfloat16)
    grad_proj_in = inner_dot(normed2_b, grad_proj_b)
    piece_grad, grad_gain2 = norm2_back(outer_dot(grad_proj_b, proj_in))
    grad1 = grad2 + piece_grad
    piece_grad, grad_gain1, grad_up1, grad_down1 = ffn_backward(
        0.5 * grad1, kept_first, up_first, down_first
    )
    grad_zero_b = (grad1 + piece_grad).astype(jnp.bfloat16)
    grad_stem = inner_dot(grad_zero_b, stacked)
    grad_stacked = row_dot(grad_zero_b, stem_full)
    freq_float = freq_keep.astype(jnp.float32)
    time_float = time_keep.astype(jnp.float32)
    input_long = (
        grad_stacked[:long_rows].reshape(4 * long_rows, mel_bins) * freq_float[None, :]
    ).astype(jnp.bfloat16)
    input_short = (
        grad_stacked[long_rows:].reshape(4 * short_rows, mel_bins)
        * freq_float[None, :]
        * time_float[:, None]
    ).astype(jnp.bfloat16)
    grad_rate = grad_rate_short + lax.dynamic_update_slice_in_dim(
        jnp.zeros_like(log_rate), grad_rate_carry + grad_rate_long, offset, 0
    )
    grad_freq = grad_freq_short + lax.dynamic_update_slice_in_dim(
        jnp.zeros_like(freq_values), grad_freq_carry + grad_freq_long, offset, 0
    )
    grad_coef = grad_coef_short + lax.dynamic_update_slice_in_dim(
        jnp.zeros_like(coef_values), grad_coef_carry + grad_coef_long, offset, 0
    )
    grad_gains = jnp.stack(
        [grad_gain1, grad_gain2, grad_gain3, grad_gain4, grad_gain_final, grad_skip], axis=1
    )
    grad_taps = grad_taps_long + grad_taps_short
    summed = (
        lax.psum_scatter(grad_stem, ("tm", "head"), scatter_dimension=0, tiled=True),
        lax.psum_scatter(grad_gains, ("tm", "head"), scatter_dimension=0, tiled=True),
        lax.psum_scatter(grad_up1, ("tm", "head"), scatter_dimension=0, tiled=True),
        lax.psum_scatter(grad_down1, ("tm", "head"), scatter_dimension=0, tiled=True),
        lax.psum_scatter(grad_proj_in, ("tm", "head"), scatter_dimension=0, tiled=True),
        lax.psum_scatter(grad_proj_out, ("tm", "head"), scatter_dimension=0, tiled=True),
        lax.psum_scatter(grad_rate, ("tm", "head"), scatter_dimension=0, tiled=True),
        lax.psum_scatter(grad_freq, ("tm", "head"), scatter_dimension=0, tiled=True),
        lax.psum_scatter(grad_coef, ("tm", "head"), scatter_dimension=0, tiled=True),
        lax.psum_scatter(grad_taps, ("tm", "head"), scatter_dimension=0, tiled=True),
        lax.psum_scatter(grad_up2, ("tm", "head"), scatter_dimension=0, tiled=True),
        lax.psum_scatter(grad_down2, ("tm", "head"), scatter_dimension=0, tiled=True),
    )
    return (
        out_long,
        out_short,
        input_long,
        input_short,
        summed[0],
        summed[1],
        summed[2],
        summed[3],
        summed[4],
        summed[5],
        summed[6],
        summed[7],
        summed[8],
        summed[9],
        summed[10],
        summed[11],
    )


def solution(mesh):
    return jax.shard_map(
        local,
        mesh=mesh,
        in_specs=(
            P(("tm", "head"), None),
            P(("tm", "head"), None),
            P(),
            P(("tm", "head"), None),
            P(("tm", "head")),
            P(("tm", "head")),
            P(("tm", "head")),
            P(("tm", "head")),
            P(("tm", "head"), None),
            P(("tm", "head"), None),
            P(("tm", "head"), None),
            P(("tm", "head"), None),
            P(("tm", "head"), None),
            P(("tm", "head"), None),
            P(("tm", "head"), None),
            P(("tm", "head"), None),
            P(("tm", "head"), None),
            P(("tm", "head"), None),
            P(("tm", "head"), None),
            P(("tm", "head"), None),
            P(("tm", "head"), None),
            P(("tm", "head"), None),
        ),
        out_specs=(
            P(("tm", "head"), None),
            P(("tm", "head"), None),
            P(("tm", "head"), None),
            P(("tm", "head"), None),
            P(("tm", "head"), None),
            P(("tm", "head"), None),
            P(("tm", "head"), None),
            P(("tm", "head"), None),
            P(("tm", "head"), None),
            P(("tm", "head"), None),
            P(("tm", "head"), None),
            P(("tm", "head"), None),
            P(("tm", "head"), None),
            P(("tm", "head"), None),
            P(("tm", "head"), None),
            P(("tm", "head"), None),
        ),
        check_vma=False,
    )
```

profile of v0, /device:TPU:0, one launch (start us, length us, event | category | flops | bytes accessed | tf_op | source)
XLA Modules:
  0.0 2919.6 jit_solution(17017643868040758380)
XLA Ops:
  16.0 44.1 %all_gather.81 = bf16[512,32]{1,0:T(8,128)(2,1)S(1)} all-gather(bf16[16,32]{1,0:T(8,128)(2,1)} %param.40), channel_id=1, replica_groups=mesh['tm'=8,'head'=4] {'tm','head'}, dimensions={0}, use_global_device_ids=true | all-gather | bytes 33792 | tf_op jit(solution)/shard_map/all_gather | solution.py:287
  60.0 37.3 %all_gather.83 = bf16[512,32]{1,0:T(8,128)(2,1)S(1)} all-gather(bf16[16,32]{1,0:T(8,128)(2,1)} %param.41), channel_id=1, replica_groups=mesh['tm'=8,'head'=4] {'tm','head'}, dimensions={0}, use_global_device_ids=true | all-gather | bytes 33792 | tf_op jit(solution)/shard_map/all_gather | solution.py:288
  97.4 38.7 %all_gather.82 = bf16[512,64]{1,0:T(8,128)(2,1)S(1)} all-gather(bf16[16,64]{1,0:T(8,128)(2,1)} %param.42), channel_id=1, replica_groups=mesh['tm'=8,'head'=4] {'tm','head'}, dimensions={0}, use_global_device_ids=true | all-gather | bytes 67584 | tf_op jit(solution)/shard_map/all_gather | solution.py:289
  147.2 36.9 %all-gather.5 = bf16[32,16,6]{1,2,0:T(8,128)(2,1)S(1)} all-gather(bf16[1,16,6]{1,2,0:T(8,128)(2,1)S(1)} %bitcast.447), channel_id=1, replica_groups=mesh['tm'=8,'head'=4] {'tm','head'}, dimensions={0}, use_global_device_ids=true | all-gather | bytes 6336 | tf_op jit(solution)/shard_map/all_gather | solution.py:282
  185.1 38.4 %all_gather.91 = bf16[512,15]{1,0:T(8,128)(2,1)S(1)} all-gather(bf16[16,15]{1,0:T(8,128)(2,1)S(1)} %copy-done.416), channel_id=1, replica_groups=mesh['tm'=8,'head'=4] {'tm','head'}, dimensions={0}, use_global_device_ids=true | all-gather | bytes 15840 | tf_op jit(solution)/shard_map/all_gather | solution.py:290
  227.3 33.0 %all-gather.2 = bf16[1024,32]{1,0:T(8,128)(2,1)} all-gather(bf16[128,32]{1,0:T(8,128)(2,1)S(1)} %get-tuple-element.551), channel_id=4, replica_groups=mesh['tm'=8,'head'=4] {'tm'}, dimensions={0}, use_global_device_ids=true | all-gather | bytes 73728 | tf_op jit(solution)/shard_map/all_gather | solution.py:41
  260.5 33.1 %all-gather.1 = bf16[1024,32]{1,0:T(8,128)(2,1)} all-gather(bf16[128,32]{1,0:T(8,128)(2,1)S(1)} %get-tuple-element.743), channel_id=3, replica_groups=mesh['tm'=8,'head'=4] {'tm'}, dimensions={0}, use_global_device_ids=true | all-gather | bytes 73728 | tf_op jit(solution)/shard_map/all_gather | solution.py:17
  293.6 32.8 %all-gather = bf16[1024,32]{1,0:T(8,128)(2,1)} all-gather(bf16[128,32]{1,0:T(8,128)(2,1)S(1)} %get-tuple-element.744), channel_id=2, replica_groups=mesh['tm'=8,'head'=4] {'tm'}, dimensions={0}, use_global_device_ids=true | all-gather | bytes 73728 | tf_op jit(solution)/shard_map/all_gather | solution.py:17
  326.4 37.9 %all_gather.76 = bf16[512,320]{1,0:T(8,128)(2,1)S(1)} all-gather(bf16[16,320]{1,0:T(8,128)(2,1)S(1)} %copy-done.392), channel_id=1, replica_groups=mesh['tm'=8,'head'=4] {'tm','head'}, dimensions={0}, use_global_device_ids=true | all-gather | bytes 337920 | tf_op jit(solution)/shard_map/all_gather | solution.py:281
  364.2 42.4 %all_gather.90 = bf16[512,512]{1,0:T(8,128)(2,1)} all-gather(bf16[16,512]{1,0:T(8,128)(2,1)S(1)} %copy-done.387), channel_id=1, replica_groups=mesh['tm'=8,'head'=4] {'tm','head'}, dimensions={0}, use_global_device_ids=true | all-gather | bytes 540672 | tf_op jit(solution)/shard_map/all_gather | solution.py:286
  446.9 32.6 %fusion.10 = (f32[512,32,33]{2,1,0:T(8,128)S(1)}, f32[512,32,33]{2,1,0:T(8,128)}) fusion(f32[512,32]{1,0:T(8,128)S(1)} %convert_element_type.380, f32[33]{0:T(128)S(1)} %copy-done.396, f32[512,32]{1,0:T(8,128)S(1)} %copy-done.105), kind=kLoop, calls=%fused_computation.26 | loop fusion | flops 2162688 | bytes 4456580 | tf_op jit(solution)/shard_map/jvp()/mul | solution.py:88
  1145.1 39.9 %all-gather.3 = bf16[1024,32]{1,0:T(8,128)(2,1)S(1)} all-gather(bf16[128,32]{1,0:T(8,128)(2,1)S(1)} %copy.674), channel_id=5, replica_groups=mesh['tm'=8,'head'=4] {'tm'}, dimensions={0}, use_global_device_ids=true | all-gather | bytes 73728 | tf_op jit(solution)/shard_map/all_gather | solution.py:41
  1392.6 48.4 %multiply_reduce_fusion.1 = (f32[512,32]{1,0:T(8,128)S(1)}, f32[512,32]{1,0:T(8,128)S(1)}, f32[512,32]{1,0:T(8,128)S(1)}, f32[512,32]{1,0:T(8,128)}, f32[512,32]...) fusion(f32[512,32,33]{2,1,0:T(8,128)} %copy-done, ...), kind=kOutput, calls=%fused_computation.48 | convolution fusion | flops 85360640 | bytes 25231360 | tf_op jit(solution)/shard_map/transpose(jvp(jcn,cnt->jtc))/dot_general | solution.py:141
  1441.0 56.8 %fusion.20 = (f32[512,32]{1,0:T(8,128)}, f32[512,32]{1,0:T(8,128)S(1)}) fusion(f32[512,32]{1,0:T(8,128)S(1)} %copy-done.102, f32[33]{0:T(128)S(1)} %copy-done.397, f32[512,32]{1,0:T(8,128)S(1)} %copy-done.106, f32[512,32,32]{2,1,0:T(8,128)} %get-tuple-element.689, f32[512,32,32]{2,1,0:T(8,128)} %rev.29, f32[512,32,1]{2,1,0:T(8,128)} %copy.619, ...), kind=kLoop, calls=%fused_computation.40 | loop fusion | flops 12943360 | bytes 17170564 | tf_op jit(solution)/shard_map/transpose(jvp())/reduce_sum | solution.py:84
  1631.3 88.5 %reduce-scatter.27.cloned.1.call-done = f32[16,32]{1,0:T(8,128)} async-done(((f32[512,32]{1,0:T(8,128)}), f32[16,32]{1,0:T(8,128)}) %reduce-scatter.27.cloned.1.call-update) | async-done | bytes 2064 | tf_op jit(solution)/shard_map/reduce_scatter | solution.py:533
  1719.8 132.3 %reduce-scatter.29.cloned.1.call-done = f32[16,32]{1,0:T(8,128)} async-done(((f32[512,32]{1,0:T(8,128)}), f32[16,32]{1,0:T(8,128)}) %reduce-scatter.29.cloned.1.call-update) | async-done | bytes 2064 | tf_op jit(solution)/shard_map/reduce_scatter | solution.py:534
  1852.0 132.0 %reduce-scatter.31.cloned.1.call-done = f32[16,64]{1,0:T(8,128)} async-done(((f32[512,64]{1,0:T(8,128)}), f32[16,64]{1,0:T(8,128)}) %reduce-scatter.31.cloned.1.call-update) | async-done | bytes 4112 | tf_op jit(solution)/shard_map/reduce_scatter | solution.py:535
  1984.1 97.9 %reduce-scatter.17.cloned.1.call-done = f32[16,320]{1,0:T(8,128)} async-done(((f32[512,320]{1,0:T(8,128)}), f32[16,320]{1,0:T(8,128)}) %reduce-scatter.17.cloned.1.call-update) | async-done | bytes 20496 | tf_op jit(solution)/shard_map/reduce_scatter | solution.py:527
  2082.0 136.7 %reduce-scatter.25.cloned.1.call-done = f32[16,512]{1,0:T(8,128)} async-done(((f32[512,512]{1,0:T(8,128)}), f32[16,512]{1,0:T(8,128)}) %reduce-scatter.25.cloned.1.call-update) | async-done | bytes 32784 | tf_op jit(solution)/shard_map/reduce_scatter | solution.py:532
  2218.6 135.4 %reduce-scatter.23.cloned.1.call-done = f32[16,1024]{1,0:T(8,128)} async-done(((f32[512,1024]{1,0:T(8,128)}), f32[16,1024]{1,0:T(8,128)}) %reduce-scatter.23.cloned.1.call-update) | async-done | bytes 65552 | tf_op jit(solution)/shard_map/reduce_scatter | solution.py:531
  2354.0 139.8 %reduce-scatter.35.cloned.1.call-done = f32[64,512]{1,0:T(8,128)} async-done(((f32[2048,512]{1,0:T(8,128)}), f32[64,512]{1,0:T(8,128)}) %reduce-scatter.35.cloned.1.call-update) | async-done | bytes 131088 | tf_op jit(solution)/shard_map/reduce_scatter | solution.py:538
  2493.8 139.6 %reduce-scatter.33.cloned.1.call-done = f32[16,2048]{1,0:T(8,128)} async-done(((f32[512,2048]{1,0:T(8,128)}), f32[16,2048]{1,0:T(8,128)}) %reduce-scatter.33.cloned.1.call-update) | async-done | bytes 131088 | tf_op jit(solution)/shard_map/reduce_scatter | solution.py:537
  2633.3 139.7 %reduce-scatter.21.cloned.1.call-done = f32[64,512]{1,0:T(8,128)} async-done(((f32[2048,512]{1,0:T(8,128)}), f32[64,512]{1,0:T(8,128)}) %reduce-scatter.21.cloned.1.call-update) | async-done | bytes 131088 | tf_op jit(solution)/shard_map/reduce_scatter | solution.py:530
  2773.1 139.6 %reduce-scatter.19.cloned.1.call-done = f32[16,2048]{1,0:T(8,128)} async-done(((f32[512,2048]{1,0:T(8,128)}), f32[16,2048]{1,0:T(8,128)}) %reduce-scatter.19.cloned.1.call-update) | async-done | bytes 131088 | tf_op jit(solution)/shard_map/reduce_scatter | solution.py:529
  (1477 shorter events, 1067.6 us)
Async XLA Ops:
  7.2 556.0 %all-gather.12.cloned.1.call-start = ((), (), s32[]{:S(2)}) async-start(), calls=%async_computation.16 | async-start | bytes 2162688 | tf_op jit(solution)/shard_map/all_gather | solution.py:283
  7.9 559.9 %all-gather.14.cloned.1.call-start = ((), (), s32[]{:S(2)}) async-start(), calls=%async_computation.17 | async-start | bytes 2162688 | tf_op jit(solution)/shard_map/all_gather | solution.py:284
  8.7 563.4 %all-gather.16.cloned.1.call-start = ((), (), s32[]{:S(2)}) async-start(), calls=%async_computation.18 | async-start | bytes 1081344 | tf_op jit(solution)/shard_map/all_gather | solution.py:285
  9.4 904.0 %all-gather.18.cloned.1.call-start = ((), (), s32[]{:S(2)}) async-start(), calls=%async_computation.19 | async-start | bytes 2162688 | tf_op jit(solution)/shard_map/all_gather | solution.py:291
  10.0 908.1 %all-gather.20.cloned.1.call-start = ((), (), s32[]{:S(2)}) async-start(), calls=%async_computation.20 | async-start | bytes 2162688 | tf_op jit(solution)/shard_map/all_gather | solution.py:292
  661.0 135.2 %all-to-all-start = ((bf16[64,4,128]{2,0,1:T(8,128)(2,1)}), bf16[64,4,128]{2,0,1:T(8,128)(2,1)}, u32[]{:S(2)}, u32[]{:S(2)}) async-start(bf16[64,4,128]{2,0,1:T(8,128)(2,1)} %copy_bitcast_fusion.3), calls=%async_computation | async-start | bytes 131072 | tf_op jit(solution)/shard_map/all_to_all | solution.py:353
  892.7 7.4 all-to-all-start.1
  904.2 6.0 collective-permute-start
  935.4 9.1 collective-permute-start.2
  938.8 5.7 collective-permute-start.3
  1034.3 102.5 %all-to-all-start.2 = ((bf16[64,4,128]{2,0,1:T(8,128)(2,1)}), bf16[64,4,128]{2,0,1:T(8,128)(2,1)S(1)}, u32[]{:S(2)}, u32[]{:S(2)}) async-start(bf16[64,4,128]{2,0,1:T(8,128)(2,1)} %copy_bitcast_fusion.2), calls=%async_computation.2 | async-start | bytes 131072 | tf_op jit(solution)/shard_map/all_to_all | solution.py:465
  1247.2 19.2 all-to-all-start.3
  1250.5 379.5 %reduce-scatter.37.cloned.1.call-start = ((), (), s32[]{:S(2)}) async-start(), calls=%async_computation.31 | async-start | bytes 270336
  1277.4 353.9 %reduce-scatter.39.cloned.1.call-start = ((), (), s32[]{:S(2)}) async-start(), calls=%async_computation.32 | async-start | bytes 270336
  1278.5 441.3 %reduce-scatter.27.cloned.1.call-start = ((), (), s32[]{:S(2)}) async-start(), calls=%async_computation.26 | async-start | bytes 270336 | tf_op jit(solution)/shard_map/reduce_scatter | solution.py:533
  1588.4 263.6 %reduce-scatter.29.cloned.1.call-start = ((), (), s32[]{:S(2)}) async-start(), calls=%async_computation.27 | async-start | bytes 270336 | tf_op jit(solution)/shard_map/reduce_scatter | solution.py:534
  1589.2 394.9 %reduce-scatter.31.cloned.1.call-start = ((), (), s32[]{:S(2)}) async-start(), calls=%async_computation.28 | async-start | bytes 270336 | tf_op jit(solution)/shard_map/reduce_scatter | solution.py:535
  1591.3 490.7 %reduce-scatter.17.cloned.1.call-start = ((), (), s32[]{:S(2)}) async-start(), calls=%async_computation.21 | async-start | bytes 811008 | tf_op jit(solution)/shard_map/reduce_scatter | solution.py:527
  1597.0 621.6 %reduce-scatter.25.cloned.1.call-start = ((), (), s32[]{:S(2)}) async-start(), calls=%async_computation.25 | async-start | bytes 1081344 | tf_op jit(solution)/shard_map/reduce_scatter | solution.py:532
  1599.8 754.2 %reduce-scatter.23.cloned.1.call-start = ((), (), s32[]{:S(2)}) async-start(), calls=%async_computation.24 | async-start | bytes 2162688 | tf_op jit(solution)/shard_map/reduce_scatter | solution.py:531
  1603.3 890.5 %reduce-scatter.35.cloned.1.call-start = ((), (), s32[]{:S(2)}) async-start(), calls=%async_computation.30 | async-start | bytes 4325376 | tf_op jit(solution)/shard_map/reduce_scatter | solution.py:538
  1608.8 1024.5 %reduce-scatter.33.cloned.1.call-start = ((), (), s32[]{:S(2)}) async-start(), calls=%async_computation.29 | async-start | bytes 4325376 | tf_op jit(solution)/shard_map/reduce_scatter | solution.py:537
  1614.9 1158.2 %reduce-scatter.21.cloned.1.call-start = ((), (), s32[]{:S(2)}) async-start(), calls=%async_computation.23 | async-start | bytes 4325376 | tf_op jit(solution)/shard_map/reduce_scatter | solution.py:530
  1620.3 1292.4 %reduce-scatter.19.cloned.1.call-start = ((), (), s32[]{:S(2)}) async-start(), calls=%async_computation.22 | async-start | bytes 4325376 | tf_op jit(solution)/shard_map/reduce_scatter | solution.py:529
  (436 other events, 8661.9 us)
Sparse Core Ops, SparseCore 0:
  10.9 59.4 all-gather.11
  73.2 55.4 all-gather.13
  131.6 52.6 all-gather.15
  187.0 56.2 all-gather.17
  246.0 56.1 all-gather.19
  1277.5 131.5 reduce-scatter.36
  1412.0 129.7 reduce-scatter.38
  1588.6 131.1 reduce-scatter.26
  1722.7 129.3 reduce-scatter.28
  1854.7 129.3 reduce-scatter.30
  1990.5 91.3 reduce-scatter.16
  2084.7 133.8 reduce-scatter.24
  2221.4 132.5 reduce-scatter.22
  2356.8 136.9 reduce-scatter.34
  2496.6 136.7 reduce-scatter.32
  2636.2 136.8 reduce-scatter.20
  2775.9 136.7 reduce-scatter.18
where the time goes:
time: 2940 us; the launch traced here: 2920 us
  waiting for transfers between devices  1290 us (44%)
  blocking collectives  506 us (17%)
  local copies, waits for them, and re-layouts  401 us (14%)
  matrix products  352 us (12%)
  other arithmetic  325 us (11%)
    reduce_scatter x1, waiting for transfers between devices, local(): lax.psum_scatter(grad_down2, ('tm', 'head'), scatter_dimension=0, tiled=T...  140 us
    reduce_scatter x1, waiting for transfers between devices, local(): lax.psum_scatter(grad_down1, ('tm', 'head'), scatter_dimension=0, tiled=T...  140 us
    reduce_scatter x1, waiting for transfers between devices, local(): lax.psum_scatter(grad_up1, ('tm', 'head'), scatter_dimension=0, tiled=True)  140 us
    reduce_scatter x1, waiting for transfers between devices, local(): lax.psum_scatter(grad_up2, ('tm', 'head'), scatter_dimension=0, tiled=True)  140 us
    reduce_scatter x1, waiting for transfers between devices, local(): lax.psum_scatter(grad_proj_out, ('tm', 'head'), scatter_dimension=0, tile...  137 us
    reduce_scatter x1, waiting for transfers between devices, local(): lax.psum_scatter(grad_proj_in, ('tm', 'head'), scatter_dimension=0, tiled...  135 us
    reduce_scatter x1, waiting for transfers between devices, local(): lax.psum_scatter(grad_freq, ('tm', 'head'), scatter_dimension=0, tiled=True)  132 us
    reduce_scatter x1, waiting for transfers between devices, local(): lax.psum_scatter(grad_coef, ('tm', 'head'), scatter_dimension=0, tiled=True)  132 us
  transfers between devices with their start and end apart: 25, of which 11 were waited for; matrix products, arithmetic and copies ran while one was open for 31% of the time, Pallas kernels for 0%

commit v1 on v0

v1 whole, which is shorter than its diff:
```python
from functools import partial

import jax
import jax.numpy as jnp
from jax import lax
from jax.experimental import pallas as pl
from jax.experimental.pallas import tpu as pltpu
from jax.sharding import PartitionSpec as P

GROUP = 32
LAGS = 192
TILE = 8
LANES = 256
SMALL_ROWS = 32
AXES = ("tm", "head")

f32 = jnp.float32
bf16 = jnp.bfloat16


def bits_of(axis):
    return (lax.axis_size(axis) - 1).bit_length()


def grid_of():
    tm, head = lax.axis_size("tm"), lax.axis_size("head")
    y = 1 << ((bits_of("tm") - 1) // 2)
    return tm // y, y, head // 2, 2


def places():
    _, y, x, _ = grid_of()
    names = [("tm", b) for b in reversed(range(y.bit_length() - 1))]
    return names + [("head", b) for b in reversed(range(bits_of("head")))]


def bit_order(first):
    heads = [n for n in places() if n[0] == "head" and n[1] > 0]
    tms = [n for n in places() if n[0] == "tm"]
    return heads + tms if first == "x" else tms + heads


def my_bit(name):
    return (lax.axis_index(name[0]) >> name[1]) & 1


def swap(value, name):
    axis, bit = name
    return lax.ppermute(value, axis, [(i, i ^ (1 << bit)) for i in range(lax.axis_size(axis))])


def send_along_z(value, hops):
    z, y, _, _ = grid_of()
    pairs = [(i, (i // y + hops) % z * y + i % y) for i in range(z * y)]
    return lax.ppermute(value, "tm", pairs)


def my_z():
    return lax.axis_index("tm") // grid_of()[1]


def joined_at(dim, mine, other, place):
    shape = mine.shape[:dim] + (2,) + mine.shape[dim:]
    index = lax.broadcasted_iota(jnp.int32, shape, dim)
    wide = lambda v: jnp.broadcast_to(jnp.expand_dims(v, dim), shape)
    return jnp.where(index == place, wide(mine), wide(other))


def tied(first, then):
    return lax.optimization_barrier((first, then))


def stacked_along_z(got):
    z = len(got)
    index = lax.broadcasted_iota(jnp.int32, (z,) + got[0].shape, 0)
    held = jnp.broadcast_to(got[0], index.shape)
    for hops in range(1, z):
        held = jnp.where(index == (my_z() - hops) % z, got[hops], held)
    return held


def pick(array, index):
    starts = [jnp.int32(0) if i is None else i for i in index]
    sizes = [n if i is None else 1 for n, i in zip(array.shape, index)]
    kept = [n for n, i in zip(array.shape, index) if i is None]
    tail = list(array.shape[len(index) :])
    starts += [jnp.int32(0)] * len(tail)
    return lax.dynamic_slice(array, starts, sizes + tail).reshape(kept + tail).astype(f32)


def settle(fold, values):
    newest, values = tied([terms[-1][0] for terms in fold.terms], values)
    for terms, array in zip(fold.terms, newest):
        terms[-1] = (array, terms[-1][1])
    return values


def all_bits():
    bits = [("tm", b) for b in reversed(range(bits_of("tm")))]
    return bits + [("head", b) for b in reversed(range(bits_of("head")))]


class Folding:
    last = None

    def __init__(self, grads, join=None):
        names = all_bits()
        self.high = [n for n in names if n[0] == "tm" and n not in places()]
        self.terms = [[(g.reshape((2,) * len(names) + g.shape[1:]), names)] for g in grads]
        firsts = "y" if len(grads) == 1 else "xy"
        self.todo = [[("head", 0)] + bit_order(first) for first in firsts]
        if join is None:
            self.todo = [todo + self.high[::-1] for todo in self.todo]
        self.fixed = [{} for _ in grads]
        self.join = join
        self.done = False

    def total(self, color, fixed):
        value = None
        for array, names in self.terms[color]:
            piece = pick(array, [fixed.get(name) for name in names])
            value = piece if value is None else value + piece
        return value

    def at_z(self, color, z):
        bits = {name: (z >> place) & 1 for place, name in enumerate(self.high[::-1])}
        return self.total(color, {**self.fixed[color], **bits})

    def load(self):
        if Folding.last is not None:
            newest = [terms[-1][0] for terms in self.terms]
            newest = tied(Folding.last, newest)[1]
            for terms, array in zip(self.terms, newest):
                terms[-1] = (array, terms[-1][1])
        colors = range(len(self.terms))
        values = []
        if self.todo[0]:
            for color in colors:
                name = self.todo[color][0]
                fixed = {**self.fixed[color], name: 1 - my_bit(name)}
                values.append(self.total(color, fixed).astype(bf16))
        elif self.join is not None:
            z = grid_of()[0]
            for hops in range(1, z):
                parts = [self.at_z(c, (my_z() + hops) % z).astype(bf16) for c in colors]
                values.append(jnp.concatenate(parts, axis=self.join))
        Folding.last = values or None
        return values

    def send(self, values):
        if self.todo[0]:
            for color, value in enumerate(values):
                name = self.todo[color].pop(0)
                got = swap(value, name)
                self.fixed[color][name] = my_bit(name)
                left = [n for n in all_bits() if n not in self.fixed[color]]
                self.terms[color].append((got, left))
        else:
            self.got = [send_along_z(v, hops + 1).astype(f32) for hops, v in enumerate(values)]
            self.done = True
        if self.join is None:
            self.done = not self.todo[0]

    def result(self):
        while not self.done:
            advance([self])
        if self.join is None:
            return [self.total(c, self.fixed[c]) for c in range(len(self.terms))]
        sums = [self.at_z(c, my_z()) for c in range(len(self.terms))]
        if len(sums) == 1:
            return [sums[0] + sum(self.got)]
        cut = sums[0].shape[self.join]
        for got in self.got:
            pieces = (got[:cut], got[cut:]) if self.join == 0 else (got[:, :cut], got[:, cut:])
            sums = [a + b for a, b in zip(sums, pieces)]
        return sums


def advance(folds, values=()):
    for fold in folds:
        if not fold.done:
            load, values = tied(fold.load(), values)
            fold.send(load)
    return values


def exchange(rows):
    return lax.all_to_all(rows, AXES, split_axis=0, concat_axis=0, tiled=True)


def edges(x, width):
    size = lax.axis_size("tm") * lax.axis_size("head")
    up = [(i, i + 1) for i in range(size - 1)]
    down = [(j, i) for i, j in up]
    before = lax.ppermute(x[x.shape[0] - width :], AXES, up)
    after = lax.ppermute(x[:width], AXES, down)
    return before, after


def row_dot(a, b):
    return jnp.dot(a, b, preferred_element_type=f32)


def inner_dot(a, b):
    return lax.dot_general(a, b, (((0,), (0,)), ((), ())), preferred_element_type=f32)


def outer_dot(a, b):
    return lax.dot_general(a, b, (((1,), (1,)), ((), ())), preferred_element_type=f32)


def norm(values):
    centred = values - jnp.mean(values, axis=-1, keepdims=True)
    scale = lax.rsqrt(jnp.mean(centred * centred, axis=-1, keepdims=True) + 1e-05)
    return centred * scale, scale


def norm_back(grad, gain, hat, scale):
    e = grad * gain
    back = e - jnp.mean(e, axis=-1, keepdims=True)
    back = (back - hat * jnp.mean(e * hat, axis=-1, keepdims=True)) * scale
    return back, jnp.sum(grad * hat, axis=0)


def silu_slope(values):
    logistic = jax.nn.sigmoid(values)
    return logistic * (1.0 + values * (1.0 - logistic))


def ffn_forward(residual, gain, up, down):
    hat, scale = norm(residual)
    normed = (hat * gain).astype(bf16)
    hidden = jnp.concatenate([row_dot(normed, part) for part in up], axis=1)
    active = jax.nn.silu(hidden).astype(bf16)
    return row_dot(active, down), (normed, hidden, active, hat, scale)


def column_blocks(x, width):
    return [x[:, i : i + width] for i in range(0, x.shape[1], width)]


def back_through(grad, parts):
    blocks = column_blocks(grad, grad.shape[1] // len(parts))
    return sum(outer_dot(block, part) for block, part in zip(blocks, parts))


def hidden_grad(grad_b, kept, down):
    return (outer_dot(grad_b, down) * silu_slope(kept[1])).astype(bf16)


def utterance_edges(groups, lead, blocks, block):
    first = jnp.int32(0)
    after = jnp.int32(lead)
    begin = jnp.int32(lead)
    for u in range(groups.shape[1]):
        end = begin + groups[0, u]
        inside = block >= begin
        first = jnp.where(inside, begin, first)
        after = jnp.where(inside, end, after)
        begin = end
    return first, after


def lag_tile(table, shift, tile):
    if isinstance(tile, int):
        return table[shift, tile * TILE : (tile + 1) * TILE, :]
    return table[shift, pl.ds(pl.multiple_of(tile * TILE, TILE), TILE), :]


def mix_forward_kernel(lead, groups, source, taps, out, rows_f, padded, table):
    blocks = source.shape[0] // GROUP
    tiles = GROUP // TILE
    rows_f[...] = source[...].astype(f32)
    padded[0:TILE, :] = jnp.zeros((TILE, padded.shape[1]), f32)
    padded[TILE:, :] = taps[...]
    for q in range(TILE):
        table[q] = padded[TILE - q : TILE - q + LAGS, :]

    def tile_of(ref, block, i):
        return ref[pl.ds(pl.multiple_of(block * GROUP + i * TILE, TILE), TILE), :]

    def one(block, carry):
        first, _ = utterance_edges(groups, lead, blocks, block)
        sums = [jnp.zeros((TILE, rows_f.shape[1]), f32) for _ in range(tiles)]
        own = [tile_of(rows_f, block, j) for j in range(tiles)]
        for q in range(TILE):
            lags = [lag_tile(table, q, d) for d in range(tiles)]
            for j in range(tiles):
                row = own[j][q : q + 1, :]
                for i in range(j, tiles):
                    sums[i] = sums[i] + lags[i - j] * row

        def pair(other, sums):
            sums = list(sums)
            base = (block - other) * tiles
            own = [tile_of(rows_f, other, j) for j in range(tiles)]
            for q in range(TILE):
                lags = {d: lag_tile(table, q, base + d) for d in range(1 - tiles, tiles)}
                for j in range(tiles):
                    row = own[j][q : q + 1, :]
                    for i in range(tiles):
                        sums[i] = sums[i] + lags[i - j] * row
            return tuple(sums)

        sums = lax.fori_loop(first, block, pair, tuple(sums))
        for i in range(tiles):
            out[pl.ds(pl.multiple_of(block * GROUP + i * TILE, TILE), TILE), :] = sums[i]
        return carry

    lax.fori_loop(0, blocks, one, 0)


def mix_backward_kernel(
    lead, groups, grad, source, taps_flipped, out, grad_taps, grad_f, rows_f, padded, table, sums_q
):
    blocks = source.shape[0] // GROUP
    tiles = GROUP // TILE
    top = LAGS // TILE - 1
    grad_f[...] = grad[...].astype(f32)
    rows_f[...] = source[...].astype(f32)
    padded[0:LAGS, :] = taps_flipped[...]
    padded[LAGS:, :] = jnp.zeros((TILE, padded.shape[1]), f32)
    for q in range(TILE):
        table[q] = padded[q : q + LAGS, :]
        sums_q[q] = jnp.zeros(sums_q.shape[1:], f32)

    def tile_of(ref, block, i):
        return ref[pl.ds(pl.multiple_of(block * GROUP + i * TILE, TILE), TILE), :]

    def add_to(q, tile, value):
        if isinstance(tile, int):
            place = slice(tile * TILE, (tile + 1) * TILE)
        else:
            place = pl.ds(pl.multiple_of(tile * TILE, TILE), TILE)
        sums_q[q, place, :] = sums_q[q, place, :] + value

    def one(block, carry):
        _, after = utterance_edges(groups, lead, blocks, block)
        sums = [jnp.zeros((TILE, rows_f.shape[1]), f32) for _ in range(tiles)]
        own = [tile_of(rows_f, block, j) for j in range(tiles)]
        here = [tile_of(grad_f, block, i) for i in range(tiles)]
        for q in range(TILE):
            lags = [lag_tile(table, TILE - 1 - q, top - d) for d in range(tiles)]
            for i in range(tiles):
                row = here[i][q : q + 1, :]
                for j in range(i + 1):
                    sums[j] = sums[j] + lags[i - j] * row
            rows = [own[j][q : q + 1, :] for j in range(tiles)]
            for d in range(tiles):
                total = here[d] * rows[0]
                for j in range(1, tiles - d):
                    total = total + here[d + j] * rows[j]
                add_to(q, d, total)

        def pair(other, sums):
            sums = list(sums)
            base = (other - block) * tiles
            here = [tile_of(grad_f, other, i) for i in range(tiles)]
            for q in range(TILE):
                lags = {
                    d: lag_tile(table, TILE - 1 - q, top - base - d)
                    for d in range(1 - tiles, tiles)
                }
                for i in range(tiles):
                    row = here[i][q : q + 1, :]
                    for j in range(tiles):
                        sums[j] = sums[j] + lags[i - j] * row
                rows = [own[j][q : q + 1, :] for j in range(tiles)]
                for d in range(1 - tiles, tiles):
                    total = None
                    for j in range(tiles):
                        if 0 <= j + d < tiles:
                            term = here[j + d] * rows[j]
                            total = term if total is None else total + term
                    add_to(q, base + d, total)
            return tuple(sums)

        sums = lax.fori_loop(block + 1, after, pair, tuple(sums))
        for j in range(tiles):
            out[pl.ds(pl.multiple_of(block * GROUP + j * TILE, TILE), TILE), :] = sums[j]
        return carry

    lax.fori_loop(0, blocks, one, 0)
    total = sums_q[0, 0:LAGS, :]
    for q in range(1, TILE):
        total = total + sums_q[q, q : q + LAGS, :]
    grad_taps[...] = total


def mixer_params():
    return pltpu.CompilerParams(vmem_limit_bytes=40 * 1024 * 1024)


def mix_forward(lead, groups, source, taps):
    rows, features = source.shape
    lanes = min(LANES, features)
    column = lambda count: pl.BlockSpec((count, lanes), lambda i: (0, i))
    return pl.pallas_call(
        partial(mix_forward_kernel, lead),
        out_shape=jax.ShapeDtypeStruct((rows, features), f32),
        grid=(features // lanes,),
        in_specs=[pl.BlockSpec(memory_space=pltpu.SMEM), column(rows), column(LAGS)],
        out_specs=column(rows),
        scratch_shapes=[
            pltpu.VMEM((rows, lanes), f32),
            pltpu.VMEM((LAGS + TILE, lanes), f32),
            pltpu.VMEM((TILE, LAGS, lanes), f32),
        ],
        compiler_params=mixer_params(),
        cost_estimate=pl.CostEstimate(
            flops=30000 * rows * features, bytes_accessed=rows * features * 8, transcendentals=0
        ),
        name="mix_forward",
    )(groups, source, taps)


def mix_backward(lead, groups, grad, source, taps_flipped, begin, width, into=None):
    rows, features = source.shape
    column = lambda count: pl.BlockSpec((count, width), lambda i: (0, begin))
    kept = [] if into is None else list(into)
    kernel = partial(mix_backward_kernel, lead)

    def body(*refs):
        kernel(*refs[:4], *refs[4 + len(kept) :])

    return pl.pallas_call(
        body,
        out_shape=(
            jax.ShapeDtypeStruct((rows, features), f32),
            jax.ShapeDtypeStruct((LAGS, features), f32),
        ),
        grid=(1,),
        in_specs=[
            pl.BlockSpec(memory_space=pltpu.SMEM),
            column(rows),
            column(rows),
            column(LAGS),
        ]
        + [pl.BlockSpec(memory_space=pl.ANY)] * len(kept),
        out_specs=(column(rows), column(LAGS)),
        scratch_shapes=[
            pltpu.VMEM((rows, width), f32),
            pltpu.VMEM((rows, width), f32),
            pltpu.VMEM((LAGS + TILE, width), f32),
            pltpu.VMEM((TILE, LAGS, width), f32),
            pltpu.VMEM((TILE, LAGS + TILE, width), f32),
        ],
        input_output_aliases={4 + i: i for i in range(len(kept))},
        compiler_params=mixer_params(),
        cost_estimate=pl.CostEstimate(
            flops=10000 * rows * width, bytes_accessed=rows * width * 8, transcendentals=0
        ),
        name="mix_backward",
    )(groups, grad, source, taps_flipped, *kept)


def fill_window(window, rows, before, after, lead, groups, block, blocks):
    first, stop = utterance_edges(groups, lead, blocks, block)
    place = lambda start, count: pl.ds(pl.multiple_of(start, 2 * TILE), count)
    window[TILE : TILE + GROUP, :] = rows[place(block * GROUP, GROUP), :].astype(f32)
    empty = jnp.zeros((TILE, window.shape[1]), f32)
    start = jnp.maximum(block * GROUP - 2 * TILE, 0)
    left = rows[place(start, 2 * TILE), :].astype(f32)[TILE:]
    left = jnp.where(block == 0, before[...].astype(f32), left)
    window[0:TILE, :] = jnp.where((block == 0) | (block > first), left, empty)
    start = jnp.minimum((block + 1) * GROUP, (blocks - 1) * GROUP)
    right = rows[place(start, 2 * TILE), :].astype(f32)[:TILE]
    right = jnp.where(block == lead - 1, after[...].astype(f32), right)
    keep = (block == lead - 1) | (block + 1 < stop)
    window[TILE + GROUP :, :] = jnp.where(keep, right, empty)


def conv_forward_kernel(lead, count, groups, rows, before, after, taps, out, window):
    blocks = rows.shape[0] // GROUP
    shift = TILE - count // 2

    def one(block, carry):
        fill_window(window, rows, before, after, lead, groups, block, blocks)
        total = None
        for k in range(count):
            term = window[shift + k : shift + k + GROUP, :] * taps[k : k + 1, :]
            total = term if total is None else total + term
        out[pl.ds(pl.multiple_of(block * GROUP, GROUP), GROUP), :] = total
        return carry

    lax.fori_loop(0, blocks, one, 0)


def conv_backward_kernel(
    lead, count, groups, grads, g_before, g_after, rows, before, after, taps, out, grad_taps,
    g_window, window, sums,
):
    blocks = rows.shape[0] // GROUP
    shift = TILE - count // 2
    sums[...] = jnp.zeros(sums.shape, f32)

    def one(block, carry):
        fill_window(g_window, grads, g_before, g_after, lead, groups, block, blocks)
        fill_window(window, rows, before, after, lead, groups, block, blocks)
        here = g_window[TILE : TILE + GROUP, :]
        total = None
        for k in range(count):
            lag = shift + count - 1 - k
            term = g_window[lag : lag + GROUP, :] * taps[k : k + 1, :]
            total = term if total is None else total + term
            product = here * window[shift + k : shift + k + GROUP, :]
            part = product[0:TILE]
            for i in range(TILE, GROUP, TILE):
                part = part + product[i : i + TILE]
            sums[k] = sums[k] + part
        out[pl.ds(pl.multiple_of(block * GROUP, GROUP), GROUP), :] = total
        return carry

    lax.fori_loop(0, blocks, one, 0)
    below = grad_taps.shape[0] - TILE - count
    grad_taps[...] = jnp.concatenate(
        [jnp.zeros((TILE, grad_taps.shape[1]), f32)]
        + [jnp.sum(sums[k], axis=0, keepdims=True) for k in range(count)]
        + [jnp.zeros((below, grad_taps.shape[1]), f32)],
        axis=0,
    )


def conv_call(kernel, lead, groups, arrays, outs, scratch, name):
    lanes = min(LANES, arrays[0].shape[1])
    column = lambda count: pl.BlockSpec((count, lanes), lambda i: (0, i))
    rows, features = arrays[0].shape
    return pl.pallas_call(
        kernel,
        out_shape=tuple(jax.ShapeDtypeStruct((n, features), f32) for n in outs),
        grid=(features // lanes,),
        in_specs=[pl.BlockSpec(memory_space=pltpu.SMEM)] + [column(a.shape[0]) for a in arrays],
        out_specs=tuple(column(n) for n in outs),
        scratch_shapes=[pltpu.VMEM(shape + (lanes,), f32) for shape in scratch],
        compiler_params=mixer_params(),
        cost_estimate=pl.CostEstimate(
            flops=4000 * rows * features, bytes_accessed=rows * features * 8, transcendentals=0
        ),
        name=name,
    )(groups, *arrays)


def conv_forward(lead, count, groups, rows, rim, taps):
    return conv_call(
        partial(conv_forward_kernel, lead, count),
        lead,
        groups,
        [rows, *rim, taps],
        [rows.shape[0]],
        [(GROUP + 2 * TILE,)],
        "conv_forward",
    )[0]


def conv_backward(lead, count, groups, grads, g_rim, rows, rim, taps):
    return conv_call(
        partial(conv_backward_kernel, lead, count),
        lead,
        groups,
        [grads, *g_rim, rows, *rim, taps],
        [rows.shape[0], SMALL_ROWS],
        [(GROUP + 2 * TILE,), (GROUP + 2 * TILE,), (count, TILE)],
        "conv_backward",
    )


def stack_rows(pieces, lanes):
    pieces = list(pieces)
    if any(p.shape[0] % 16 for p in pieces):
        fill = lambda p: jnp.pad(p, ((0, 0), (0, lanes - p.shape[1])))
        blocks = [b for p in pieces for b in (column_blocks(p, lanes) if p.shape[1] > lanes else [p])]
        return jnp.concatenate([fill(b) for b in blocks], axis=0)
    total = sum(p.shape[0] * -(-p.shape[1] // lanes) for p in pieces)

    def kernel(*refs):
        out, row = refs[-1], 0
        for ref in refs[:-1]:
            count, width = ref.shape
            for begin in range(0, width, lanes):
                here = min(lanes, width - begin)
                if here < lanes:
                    out[row : row + count, :] = jnp.zeros((count, lanes), out.dtype)
                out[row : row + count, 0:here] = ref[:, begin : begin + here]
                row += count

    return pl.pallas_call(
        kernel,
        out_shape=jax.ShapeDtypeStruct((total, lanes), pieces[0].dtype),
        in_specs=[pl.BlockSpec(memory_space=pltpu.VMEM)] * len(pieces),
        out_specs=pl.BlockSpec(memory_space=pltpu.VMEM),
        compiler_params=mixer_params(),
        name="stack_rows",
    )(*pieces)


def cmul(a, b):
    return (a[0] * b[0] - a[1] * b[1], a[0] * b[1] + a[1] * b[0])


def powers(rate, freq, steps):
    decay = jnp.exp(-rate * steps)
    return decay * jnp.cos(freq * steps), decay * jnp.sin(freq * steps)


def shifted(x, count):
    pad = jnp.zeros((abs(count),) + x.shape[1:], x.dtype)
    if count > 0:
        return jnp.concatenate([pad, x[:-count]], axis=0)
    return jnp.concatenate([x[-count:], pad], axis=0)


def chunk_scan(values, decay, sign):
    count = values[0].shape[0]
    hop = 1
    while hop < count:
        moved = tuple(shifted(v, sign * hop) for v in values)
        added = cmul(decay, moved)
        values = (values[0] + added[0], values[1] + added[1])
        decay = cmul(decay, decay)
        hop *= 2
    return values


def long_tables(log_rate, freq, coef, chunk):
    channels, states = log_rate.shape
    lanes = channels * states
    rate = jnp.exp(log_rate).reshape(1, lanes)
    freq = freq.reshape(1, lanes)
    scale = jnp.sqrt(2.0 * rate)
    weight = (
        scale * coef[:, :states].reshape(1, lanes),
        scale * coef[:, states:].reshape(1, lanes),
    )
    steps = jnp.arange(chunk + 1).astype(f32)[:, None]
    power = powers(rate, freq, steps)
    mask = jnp.arange(channels)[:, None] == (jnp.arange(lanes) // states)[None, :]
    mask = mask.astype(f32)[:, None, :]

    def spread(pair):
        wide = [(mask * part[None]).reshape(channels * chunk, lanes) for part in pair]
        return jnp.concatenate(wide, axis=1).astype(bf16)

    ages = tuple(p[:chunk][::-1] for p in power)
    leads = tuple(p[1:] for p in power)
    weighted = lambda pair: cmul(weight, pair)
    signed = lambda pair: (pair[0], -pair[1])
    return {
        "ages": spread(ages),
        "ages_slope": spread(tuple(a * steps[:chunk][::-1] for a in ages)),
        "leads": spread(leads),
        "leads_slope": spread(tuple(a * steps[1:] for a in leads)),
        "read": spread(signed(weighted(leads))),
        "read_back": spread(signed(weighted(ages))),
        "decay": powers(rate, freq, jnp.float32(chunk)),
        "rate": rate,
        "scale": scale,
        "weight": weight,
    }


def halves(x):
    lanes = x.shape[1] // 2
    return x[:, :lanes], x[:, lanes:]


def long_forward(rows, tables):
    added = halves(row_dot(rows, tables["ages"]))
    state = chunk_scan(added, tables["decay"], 1)
    before = tuple(shifted(v, 1) for v in state)
    carried = outer_dot(jnp.concatenate(before, axis=1).astype(bf16), tables["read"])
    return carried, before


def long_backward(grads, tables):
    read = halves(row_dot(grads, tables["leads"]))
    future = chunk_scan(read, tables["decay"], -1)
    later = tuple(shifted(v, -1) for v in future)
    return outer_dot(jnp.concatenate(later, axis=1).astype(bf16), tables["read_back"])


def long_moments(rows, grads, tables, before, chunk):
    added = halves(row_dot(rows, tables["ages_slope"]))
    late = cmul(tables["decay"], before)
    added = tuple(a + chunk * b for a, b in zip(added, late))
    slope_before = tuple(shifted(v, 1) for v in chunk_scan(added, tables["decay"], 1))
    read = halves(row_dot(grads, tables["leads"]))
    slope = halves(row_dot(grads, tables["leads_slope"]))
    total = lambda pair: tuple(jnp.sum(v, axis=0, keepdims=True) for v in pair)
    moment = total(cmul(read, before))
    first = cmul(slope, before)
    second = cmul(read, slope_before)
    return moment, total((first[0] + second[0], first[1] + second[1]))


def lag_values(log_rate, freq, coef, lags):
    states = log_rate.shape[1]
    rate = jnp.exp(log_rate)
    scale = jnp.sqrt(2.0 * rate)
    steps = jnp.arange(lags).astype(f32)
    real, imaginary = powers(rate[:, :, None], freq[:, :, None], steps)
    weights = (scale * coef[:, :states], scale * coef[:, states:])
    taps = jnp.sum(weights[0][:, :, None] * real - weights[1][:, :, None] * imaginary, axis=1)
    return taps, (real, imaginary)


def local(*args):
    Folding.last = None
    return layer(*args)


def layer(
    feats_long,
    feats_short,
    long_length,
    short_groups,
    freq_start,
    freq_width,
    time_start,
    time_width,
    stem_weight,
    norm_gains,
    ffn1_up,
    ffn1_down,
    mixer_in,
    mixer_out,
    mixer_log_rate,
    mixer_freq,
    mixer_coef,
    conv_taps,
    ffn2_up,
    ffn2_down,
    cotangent_long,
    cotangent_short,
):
    devices = lax.axis_size("tm") * lax.axis_size("head")
    own = stem_weight.shape[0]
    features = own * devices
    hidden_width = ffn1_up.shape[1]
    mel_bins = feats_long.shape[1]
    stem_width = stem_weight.shape[1]
    gain_count, tap_count = norm_gains.shape[1], conv_taps.shape[1]
    down_rows = ffn1_down.shape[0]
    up_blocks = hidden_width // features
    long_rows = feats_long.shape[0] // 4
    short_rows = feats_short.shape[0] // 4
    lead = long_rows // GROUP
    padded_to = lambda w, lanes: jnp.pad(w, ((0, 0), (0, lanes - w.shape[1])))

    block = stack_rows(
        [ffn1_up, mixer_in[:, :features], ffn1_down, stem_weight], features
    )
    split = own * (up_blocks + 1)
    got = [block] + [send_along_z(block, hops) for hops in range(1, grid_of()[0])]
    held = [
        stacked_along_z([g[:split] for g in got]),
        stacked_along_z([g[split:] for g in got]),
    ]
    back = stack_rows([ffn2_up, ffn2_down, mixer_out, mixer_in[:, features:]], features)

    held, mixer_params_own = tied(held, (mixer_log_rate, mixer_freq, mixer_coef))
    log_rate, freq_values, coef_values = (p.astype(f32) for p in mixer_params_own)
    own_taps, lag_powers = lag_values(log_rate, freq_values, coef_values, LAGS)
    shared = jnp.concatenate([own_taps.astype(bf16), norm_gains, conv_taps], axis=1)
    shared = padded_to(shared, -(-shared.shape[1] // 128) * 128)
    shared = exchange(jnp.broadcast_to(shared, (devices,) + shared.shape))

    dims = [[], []]
    orders = [bit_order("x"), bit_order("y")]
    tables_in = (log_rate, freq_values, coef_values)
    for step in range(len(orders[0])):
        for color in range(2):
            name = orders[color][step]
            other = swap(held[color], name)
            dims[color] = [n for n in places() if n in dims[color] or n == name]
            held[color] = joined_at(
                1 + dims[color].index(name), held[color], other, my_bit(name)
            )
        if step == 0:
            held, (tables_in, back) = tied(held, (tables_in, back))
    back_full = lax.all_gather(back, AXES, axis=0)
    tables = long_tables(*tables_in, long_rows)
    core = ("head", 0)
    other = [swap(h, core) for h in held]

    def assembled(color, begin, count, lanes=features):
        part = lambda v: v[..., begin : begin + count, :lanes]
        full = joined_at(1 + len(dims[color]), part(held[color]), part(other[color]), my_bit(core))
        return full.reshape(-1, lanes)

    up_first = [assembled(0, i * own, own) for i in range(up_blocks)]
    proj_inner = assembled(0, up_blocks * own, own)
    down_first = assembled(1, 0, down_rows)
    stem_full = assembled(1, down_rows, own)

    shared = shared.reshape(features, -1).astype(f32).T
    lag_taps = shared[:LAGS]
    lag_flipped = lag_taps[::-1]
    gains = shared[LAGS : LAGS + gain_count]
    taps = padded_to(shared[LAGS + gain_count : LAGS + gain_count + tap_count].T, 16).T

    mel_index = jnp.arange(mel_bins)
    mel_band = (mel_index >= freq_start[0]) & (mel_index < freq_start[0] + freq_width[0])
    freq_keep = (1 - mel_band.astype(jnp.int32)).astype(bf16)
    row_index = jnp.arange(4 * short_rows)
    time_blank = (row_index >= time_start[0]) & (row_index < time_start[0] + time_width[0])
    time_keep = (1 - time_blank.astype(jnp.int32)).astype(bf16)
    stacked = jnp.concatenate(
        [
            (feats_long * freq_keep[None, :]).reshape(long_rows, 4 * mel_bins),
            (feats_short * freq_keep[None, :] * time_keep[:, None]).reshape(
                short_rows, 4 * mel_bins
            ),
        ],
        axis=0,
    )
    stacked = padded_to(stacked, features)
    position = lax.axis_index(AXES) * long_rows + jnp.arange(long_rows)
    valid_long = (position < long_length[0]).astype(f32)
    valid = jnp.concatenate([valid_long, jnp.ones((short_rows,), f32)])[:, None]
    valid_b = valid.astype(bf16)

    residual = outer_dot(stacked, stem_full)
    ffn_first, kept_first = ffn_forward(residual, gains[0], up_first, down_first)
    residual1 = residual + 0.5 * ffn_first
    hat2, scale2 = norm(residual1)
    normed2 = (hat2 * gains[1]).astype(bf16)
    inputs_b = row_dot(normed2, proj_inner).astype(bf16)
    source_b = inputs_b * valid_b

    def to_owner(rows):
        return rows.T.reshape(devices, 8, own * long_rows // 8)

    def at_owner(rows):
        return exchange(rows).reshape(devices, own * long_rows)

    def from_owner(rows):
        return exchange(rows.astype(bf16).reshape(devices, 8, own * long_rows // 8))

    def at_home(rows):
        return rows.reshape(features, long_rows).T.astype(f32)

    long_in, normed2 = tied(to_owner(source_b[:long_rows]), normed2)
    long_in = at_owner(long_in)
    carried, before = long_forward(long_in, tables)
    carried, source_b = tied(carried.astype(bf16), source_b)
    carried = from_owner(carried)
    mixed = mix_forward(lead, short_groups, source_b, lag_taps)
    up_second = [
        back_full[:, i : i + own].reshape(features, features)
        for i in range(0, own * up_blocks, own)
    ]
    place = own * up_blocks
    down_second = back_full[:, place : place + down_rows].reshape(hidden_width, features)
    place += down_rows
    proj_out = back_full[:, place : place + own].reshape(features, features)
    proj_gate = back_full[:, place + own :].reshape(features, features)
    gates = row_dot(normed2, proj_gate)
    gate_act = jax.nn.silu(gates)

    below = lambda v: jnp.pad(v, ((0, short_rows), (0, 0)))
    mixed = (mixed + below(at_home(carried))).astype(bf16).astype(f32)
    inputs_f = inputs_b.astype(f32)
    joined = mixed + gains[5] * inputs_f
    gated_b = (joined * gate_act).astype(bf16)

    residual2 = residual1 + row_dot(gated_b, proj_out)
    hat3, scale3 = norm(residual2)
    spread_b = (hat3 * gains[2]).astype(bf16) * valid_b
    rim = edges(spread_b[:long_rows], TILE)
    pre = conv_forward(lead, tap_count, short_groups, spread_b, rim, taps)
    residual3 = residual2 + jax.nn.silu(pre)
    ffn_second, kept_second = ffn_forward(residual3, gains[3], up_second, down_second)
    residual4 = residual3 + 0.5 * ffn_second
    hat5, scale5 = norm(residual4)
    final = (hat5 * gains[4]).astype(bf16)

    cotangent = jnp.concatenate([cotangent_long, cotangent_short], axis=0).astype(f32)
    grad4, grad_gain4 = norm_back(cotangent, gains[4], hat5, scale5)
    grad_b = (0.5 * grad4).astype(bf16)
    grad_hidden = hidden_grad(grad_b, kept_second, down_second)
    normed, _, active, hat, scale = kept_second
    by_owner = lambda g: g.astype(bf16).reshape(devices, -1, g.shape[1])
    piece, grad_gain3 = norm_back(back_through(grad_hidden, up_second), gains[3], hat, scale)
    grad3 = grad4 + piece
    grad_pre_b = (grad3 * silu_slope(pre)).astype(bf16)
    grad_pre_b, (normed, active) = tied(grad_pre_b, (normed, active))
    grad_rim = edges(grad_pre_b[:long_rows], TILE)
    second = Folding(
        [by_owner(inner_dot(normed, grad_hidden)), by_owner(inner_dot(active, grad_b))]
    )
    grad_pre_b = advance([second], grad_pre_b)
    grad_spread, small_rows = conv_backward(
        lead, tap_count, short_groups, grad_pre_b, grad_rim, spread_b, rim, taps
    )
    piece, grad_gain2 = norm_back(grad_spread * valid, gains[2], hat3, scale3)
    grad2 = grad3 + piece
    grad_out_b = advance([second], grad2.astype(bf16))
    grad_gated = outer_dot(grad_out_b, proj_out)
    grad_joined = grad_gated * gate_act
    grad_mixed_b = grad_joined.astype(bf16)
    grad_in, (grad_mixed_b, gated_b) = tied(
        to_owner(grad_mixed_b[:long_rows]), (grad_mixed_b, gated_b)
    )
    grad_in = at_owner(grad_in)
    grad_gates = grad_gated * joined * silu_slope(gates)
    grad_gain5 = jnp.sum(grad_joined * inputs_f, axis=0)
    grad_proj_out = by_owner(inner_dot(gated_b, grad_out_b))
    half = features // 2
    run = lambda grad, begin, into=None: mix_backward(
        lead, short_groups, grad, source_b, lag_flipped, begin, half, into
    )
    first_half = run(grad_mixed_b, 0)
    later = long_backward(grad_in, tables)
    later, grad_mixed_b = tied(later.astype(bf16), grad_mixed_b)
    later = from_owner(later)
    grad_mixed_b = advance([second], grad_mixed_b)
    grad_source, grad_lags = run(grad_mixed_b, 1, first_half)
    grad_source = (grad_source + below(at_home(later))).astype(bf16).astype(f32)
    grad_inner_b = (grad_source * valid + gains[5] * grad_joined).astype(bf16)
    grad_inner_b = advance([second], grad_inner_b)
    grad_gates_b = grad_gates.astype(bf16)
    back = outer_dot(grad_inner_b, proj_inner) + outer_dot(grad_gates_b, proj_gate)
    piece, grad_gain1 = norm_back(back, gains[1], hat2, scale2)
    grad1 = grad2 + piece
    grad_b = (0.5 * grad1).astype(bf16)
    normed, _, active, hat, scale = kept_first
    unit = (jnp.arange(LAGS)[:, None] == jnp.arange(features)[None, :]).astype(bf16)
    early_out = jnp.concatenate(
        [
            by_owner(inner_dot(normed2, grad_inner_b)),
            by_owner(inner_dot(normed2, grad_gates_b)),
            grad_proj_out,
            by_owner(inner_dot(grad_lags.astype(bf16), unit)),
        ],
        axis=1,
    )
    early = Folding([by_owner(inner_dot(active, grad_b)), early_out], 0)
    grad_b = advance([early], grad_b)
    grad_hidden = hidden_grad(grad_b, kept_first, down_first)
    grad_hidden = advance([second], grad_hidden)
    late = Folding([by_owner(inner_dot(normed, grad_hidden))], 0)
    grad_hidden = advance([late, early], grad_hidden)
    piece, grad_gain0 = norm_back(back_through(grad_hidden, up_first), gains[0], hat, scale)
    grad_zero_b = settle(second, advance([late], (grad1 + piece).astype(bf16)))

    row = jnp.arange(SMALL_ROWS)[:, None]
    gain_rows = [grad_gain0, grad_gain1, grad_gain2, grad_gain3, grad_gain4, grad_gain5]
    for k, grad_gain in enumerate(gain_rows):
        small_rows = jnp.where(row == k, grad_gain[None, :], small_rows)
    lane = jnp.arange(features)[None, :] - stem_width
    place = jnp.where(lane < gain_count, lane, lane - gain_count + TILE)
    small_unit = ((place == row) & (lane >= 0) & (lane < gain_count + tap_count)).astype(bf16)
    small = inner_dot(grad_zero_b, stacked) + inner_dot(small_rows.astype(bf16), small_unit)
    small = exchange(by_owner(small))
    grad_zero_b = advance([early], grad_zero_b)
    grad_stacked = row_dot(grad_zero_b, stem_full)[:, :stem_width]
    freq_float = freq_keep.astype(f32)
    time_float = time_keep.astype(f32)
    input_long = (
        grad_stacked[:long_rows].reshape(4 * long_rows, mel_bins) * freq_float[None, :]
    ).astype(bf16)
    input_short = (
        grad_stacked[long_rows:].reshape(4 * short_rows, mel_bins)
        * freq_float[None, :]
        * time_float[:, None]
    ).astype(bf16)
    moment_in, input_long, input_short = advance(
        [early, late], ((long_in, grad_in, before), input_long, input_short)
    )
    for fold in (second, early):
        while not fold.done:
            advance([fold])
    moment_in = settle(second, moment_in)
    moment, moment_slope = long_moments(*moment_in[:2], tables, moment_in[2], long_rows)
    sum_up2, sum_down2 = second.result()
    sum_early = early.result()
    grad_small = jnp.sum(small.astype(f32), axis=0)
    (sum_up1,) = late.result()
    sum_down1, rest = sum_early
    sum_in = jnp.concatenate([rest[:own], rest[own : 2 * own]], axis=1)
    sum_out = rest[2 * own : 3 * own]
    lag_grad = rest[3 * own :, :LAGS]

    states = log_rate.shape[1]
    steps = jnp.arange(LAGS).astype(f32)
    near = tuple(jnp.sum(lag_grad[:, None, :] * p, axis=2) for p in lag_powers)
    near_slope = tuple(jnp.sum((lag_grad * steps)[:, None, :] * p, axis=2) for p in lag_powers)
    shape = (own, states)
    moment = tuple(a.reshape(shape) + b for a, b in zip(moment, near))
    moment_slope = tuple(a.reshape(shape) + b for a, b in zip(moment_slope, near_slope))
    weight = tuple(w.reshape(shape) for w in tables["weight"])
    rate = tables["rate"].reshape(shape)
    scale = tables["scale"].reshape(shape)
    pulled = cmul(weight, moment)
    pulled_slope = cmul(weight, moment_slope)
    grad_rate = 0.5 * pulled[0] - rate * pulled_slope[0]
    grad_freq = -pulled_slope[1]
    grad_coef = jnp.concatenate([scale * moment[0], -scale * moment[1]], axis=1)

    return (
        final[:long_rows],
        final[long_rows:],
        input_long,
        input_short,
        grad_small[:, :stem_width],
        grad_small[:, stem_width : stem_width + gain_count],
        sum_up1,
        sum_down1,
        sum_in,
        sum_out,
        grad_rate,
        grad_freq,
        grad_coef,
        grad_small[:, stem_width + gain_count : stem_width + gain_count + tap_count],
        sum_up2,
        sum_down2,
    )


def solution(mesh):
    rows = P(AXES, None)
    flat = P(AXES)
    return jax.shard_map(
        local,
        mesh=mesh,
        in_specs=(rows, rows, P(), rows, flat, flat, flat, flat) + (rows,) * 14,
        out_specs=(rows,) * 16,
        check_vma=False,
    )
```

time: 2940 us -> 350 us (0.12)
  waiting for transfers between devices: 1290 us -> 42.6 us
  blocking collectives: 506 us -> 0 us
  local copies, waits for them, and re-layouts: 401 us -> 49.3 us
  matrix products: 352 us -> 45 us
  other arithmetic: 325 us -> 69.9 us
  starting transfers between devices: 25 us -> 87.2 us
    reduce_scatter x10 -> x0, waiting for transfers between devices: 1280 us -> none  [the longest x1 140 us: local(): lax.psum_scatter(grad_down2, ('tm', 'head'), scatter_dimension=0, tiled=T...]
    all_gather x14 -> x0, blocking collectives: 506 us -> none  [the longest x4 127 us: prefix_2(): lax.all_gather(a.astype(kind), axis)]
    dot_general x51 -> x45, matrix products: 352 us -> 45 us  [the longest x19 16.9 us: row_dot(): return jnp.dot(a, b, preferred_element_type=f32)]
    pad x90 -> x0, local copies, waits for them, and re-layouts: 124 us -> none  [group_scan(): lax.associative_scan(chain_step, (scale_real, scale_imaginary, added_real...]
    reduce_sum x26 -> x12, other arithmetic: 111 us -> 10.2 us  [the longest x1 2.97 us: layer(): jnp.sum(lag_grad[:, None, :] * p, axis=2)]
    rev x10 -> x3, local copies, waits for them, and re-layouts: 63.1 us -> 0.97 us  [the longest x1 0.76 us: layer(): lag_flipped = lag_taps[::-1]]
    ppermute x4 -> x38, starting transfers between devices: 8.17 us -> 59.1 us  [the longest x25 27.5 us: swap(): lax.ppermute(value, axis, [(i, i ^ 1 << bit) for i in range(lax.axis_size...]
    dot_general x17 -> x0, local copies, waits for them, and re-layouts: 41.7 us -> none  [the longest x4 12.1 us: group_scan(): jnp.einsum('jcn,cnt->jtc', before_imaginary, lead_imaginary, precision=hi...]
  transfers between devices with their start and end apart: 25 -> 45, of which waited for: 11 -> 10; matrix products, arithmetic and copies ran while one was open for 31% -> 33% of each run, Pallas kernels for 0% -> 7%
where the time goes in v1:
time: 350 us; the launch traced here: 343 us
  starting transfers between devices  87.2 us (25%)
  other arithmetic  69.9 us (20%)
  local copies, waits for them, and re-layouts  49.3 us (14%)
  matrix products  45 us (13%)
  waiting for transfers between devices  42.6 us (12%)
  Pallas kernels  28.1 us (8%)
  between operations  20.8 us (6%)
    all_to_all x6, starting transfers between devices, exchange(): return lax.all_to_all(rows, AXES, split_axis=0, concat_axis=0, tiled=True)  28 us
    ppermute x25, waiting for transfers between devices, swap(): lax.ppermute(value, axis, [(i, i ^ 1 << bit) for i in range(lax.axis_size...  27.8 us
    ppermute x25, starting transfers between devices, swap(): lax.ppermute(value, axis, [(i, i ^ 1 << bit) for i in range(lax.axis_size...  27.5 us
    unnamed x374, local copies, waits for them, and re-layouts  18.2 us
    dot_general x19, matrix products, row_dot(): return jnp.dot(a, b, preferred_element_type=f32)  16.9 us
    dot_general x16, matrix products, outer_dot(): lax.dot_general(a, b, (((1,), (1,)), ((), ())), preferred_element_type=f32)  16.6 us
    convert_element_type x14, other arithmetic, load(): values.append(self.total(color, fixed).astype(bf16))  16.3 us
    ppermute x9, starting transfers between devices, send_along_z(): return lax.ppermute(value, 'tm', pairs)  15.3 us
  transfers between devices with their start and end apart: 45, of which 10 were waited for; matrix products, arithmetic and copies ran while one was open for 33% of the time, Pallas kernels for 7%

profile of v1, /device:TPU:0, one launch (start us, length us, event | category | flops | bytes accessed | tf_op | source)
XLA Modules:
  0.0 343.1 jit_solution(872050281101833406)
XLA Ops:
  10.4 3.1 collective-permute-start.2
  13.4 2.6 collective-permute-start.1
  38.6 3.3 all-to-all-start
  49.0 14.0 %collective-permute-done.7 = bf16[4,2,80,512]{3,2,1,0:T(8,128)(2,1)} collective-permute-done((bf16[4,2,80,512]{3,2,1,0:T(8,128)(2,1)S(1)}, bf16[4,2,80,512]{3,2,1,0:T(8,128)(2,1)}, u32[]{:S(2)}, u32[]{:S(2)}) %collective-permute-start.7) | collective-permute-done | bytes 655392 | tf_op jit(solution)/shard_map/ppermute | solution.py:49
  66.3 5.7 %multiply_convert_fusion.5 = (bf16[16,64,512]{2,1,0:T(8,128)(2,1)}, bf16[16,64,512]{2,1,0:T(8,128)(2,1)}, bf16[16,64,512]{2,1,0:T(8,128)(2,1)}, bf16[16,64,512]{...) fusion(f32[64,512]{1,0:T(8,128)S(1)} %get-tuple-element.399, ...), kind=kLoop, calls=%fused_computation.36 | loop fusion | flops 12582912 | bytes 14188544 | tf_op jit(solution)/shard_map/convert.116
  90.2 4.4 %all-to-all-start.1 = ((bf16[32,8,128]{2,1,0:T(8,128)(2,1)}), bf16[32,8,128]{2,1,0:T(8,128)(2,1)S(1)}, u32[]{:S(2)}, u32[]{:S(2)}) async-start(bf16[32,8,128]{2,1,0:T(8,128)(2,1)} %reshape.954), calls=%async_computation.1 | async-start | bytes 131072 | tf_op jit(solution)/shard_map/all_to_all | solution.py:188
  95.5 7.5 %all-to-all-done.1 = bf16[32,8,128]{2,1,0:T(8,128)(2,1)S(1)} async-done(((bf16[32,8,128]{2,1,0:T(8,128)(2,1)}), bf16[32,8,128]{2,1,0:T(8,128)(2,1)S(1)}, u32[]{:S(2)}, u32[]{:S(2)}) %all-to-all-start.1) | async-done | bytes 65568 | tf_op jit(solution)/shard_map/all_to_all | solution.py:188
  107.7 2.8 all-to-all-start.2
  110.5 5.6 %mix_forward.1 = f32[448,512]{1,0:T(8,128)S(1)} custom-call(s32[1,4]{1,0:T(1,128)S(1)} %copy-done.6, bf16[448,512]{1,0:T(8,128)(2,1)S(1)} %get-tuple-element.132.source.refs_2_, f32[192,512]{1,0:T(8,128)S(1)} %slice.583.taps), custom_call_target="tpu_custom_call" | custom-call | flops 6881280000 | bytes 1835008 | tf_op jit(solution)/shard_map/mix_forward/pallas_call | solution.py:398
  118.2 3.2 fusion.186
  131.6 3.0 conv_forward.1
  149.9 11.8 %collective-permute-start.13 = (bf16[8,512]{1,0:T(8,128)(2,1)S(1)}, bf16[8,512]{1,0:T(8,128)(2,1)S(1)}, u32[]{:S(2)}, u32[]{:S(2)}) collective-permute-start(bf16[8,512]{1,0:T(8,128)(2,1)S(1)} %get-tuple-element.356), channel_id=1, source_target_pairs={{0,1},{1,2},{2,3},{3,4},{4,5},{5,6},{6,7},{7,8},{8,9},{9,10},{10,1... | collective-permute-start | bytes 24584 | tf_op jit(solution)/shard_map/ppermute | solution.py:195
  166.9 5.1 %conv_backward.1 = (f32[448,512]{1,0:T(8,128)S(1)}, f32[32,512]{1,0:T(8,128)S(1)}) custom-call(s32[1,4]{1,0:T(1,128)S(1)} %copy-done.6, bf16[448,512]{1,0:T(8,128)(2,1)S(1)} %get-tuple-element.143.grads, bf16[8,512]{1,0:T(8,128)(2,1)S(1)} %collective-permute-done.13.g_before, bf16[8,512]{1,0:T(8,128)(2,1)S(1)} %collective-permute-done.14.g_after, ...), custom_call_target="tpu_custom_call" | custom-call | flops 917504000 | bytes 1835008 | tf_op jit(solution)/shard_map/conv_backward/pallas_call | solution.py:528
  182.7 8.8 %all-to-all-start.3 = ((bf16[32,8,128]{2,1,0:T(8,128)(2,1)}), bf16[32,8,128]{2,1,0:T(8,128)(2,1)S(1)}, u32[]{:S(2)}, u32[]{:S(2)}) async-start(bf16[32,8,128]{2,1,0:T(8,128)(2,1)} %reshape.966), calls=%async_computation.3 | async-start | bytes 131072 | tf_op jit(solution)/shard_map/all_to_all | solution.py:188
  205.2 3.7 %all-to-all-start.4 = ((bf16[32,8,128]{2,1,0:T(8,128)(2,1)}), bf16[32,8,128]{2,1,0:T(8,128)(2,1)S(1)}, u32[]{:S(2)}, u32[]{:S(2)}) async-start(bf16[32,8,128]{2,1,0:T(8,128)(2,1)} %bitcast.283), calls=%async_computation.4 | async-start | bytes 131072 | tf_op jit(solution)/shard_map/all_to_all | solution.py:188
  210.3 6.9 %mix_backward.2 = (f32[448,512]{1,0:T(8,128)S(1)}, f32[192,512]{1,0:T(8,128)S(1)}) custom-call(s32[1,4]{1,0:T(1,128)S(1)} %copy-done.6, bf16[448,512]{1,0:T(8,128)(2,1)S(1)} %convert_element_type.1065.refs_1_, bf16[448,512]{1,0:T(8,128)(2,1)S(1)} %get-tuple-element.132.source.refs_2_, f32[192,512]{1,0:T(8,128)S(1)} %rev.13.refs_3_), custom_call_target="tpu_custom_call" | custom-call | flops 1146880000 | bytes 917504 | tf_op jit(solution)/shard_map/mix_backward/pallas_call | solution.py:426
  223.7 6.9 %mix_backward.3 = (f32[448,512]{1,0:T(8,128)S(1)}, f32[192,512]{1,0:T(8,128)S(1)}) custom-call(s32[1,4]{1,0:T(1,128)S(1)} %copy-done.6, bf16[448,512]{1,0:T(8,128)(2,1)S(1)} %convert_element_type.1065.refs_1_, bf16[448,512]{1,0:T(8,128)(2,1)S(1)} %get-tuple-element.132.source.refs_2_, ...), custom_call_target="tpu_custom_call", output_to_operand_aliasing={{0}: (4, {}), {1}: (5, {})} | custom-call | flops 1146880000 | bytes 917504 | tf_op jit(solution)/shard_map/mix_backward/pallas_call | solution.py:426
  241.5 2.6 multiply_convert_fusion
  249.7 2.5 collective-permute-start.26
  264.0 4.9 %all-to-all-start.5 = ((bf16[32,16,512]{2,1,0:T(8,128)(2,1)}), bf16[32,16,512]{2,1,0:T(8,128)(2,1)}, u32[]{:S(2)}, u32[]{:S(2)}) async-start(bf16[32,16,512]{2,1,0:T(8,128)(2,1)} %bitcast.562), calls=%async_computation.5 | async-start | bytes 1048576 | tf_op jit(solution)/shard_map/all_to_all | solution.py:188
  281.0 10.6 %collective-permute-done.28 = bf16[2,2,64,512]{3,2,1,0:T(8,128)(2,1)} collective-permute-done((bf16[2,2,64,512]{3,2,1,0:T(8,128)(2,1)}, bf16[2,2,64,512]{3,2,1,0:T(8,128)(2,1)}, u32[]{:S(2)}, u32[]{:S(2)}) %collective-permute-start.28) | collective-permute-done | bytes 262176 | tf_op jit(solution)/shard_map/ppermute | solution.py:49
  300.5 3.4 collective-permute-start.37
  317.3 3.0 multiply_reduce_fusion.19
  327.2 3.1 collective-permute-done.33
  (718 shorter events, 193.9 us)
Async XLA Ops:
  10.4 21.5 %collective-permute-start.2 = (bf16[160,512]{1,0:T(8,128)(2,1)S(1)}, bf16[160,512]{1,0:T(8,128)(2,1)S(1)}, u32[]{:S(2)}, u32[]{:S(2)}) collective-permute-start(bf16[160,512]{1,0:T(8,128)(2,1)S(1)} %stack_rows.2), channel_id=1, source_target_pairs={{0,8},{4,12},{8,16},{12,20},{16,24},{20,28},{24,0},{28,4},{1,9},{5... | collective-permute-start | bytes 491528 | tf_op jit(solution)/shard_map/ppermute | solution.py:55
  13.4 18.5 %collective-permute-start.1 = (bf16[160,512]{1,0:T(8,128)(2,1)S(1)}, bf16[160,512]{1,0:T(8,128)(2,1)S(1)}, u32[]{:S(2)}, u32[]{:S(2)}) collective-permute-start(bf16[160,512]{1,0:T(8,128)(2,1)S(1)} %stack_rows.2), channel_id=1, source_target_pairs={{0,16},{4,20},{8,24},{12,28},{16,0},{20,4},{24,8},{28,12},{1,17},{... | collective-permute-start | bytes 491528 | tf_op jit(solution)/shard_map/ppermute | solution.py:55
  16.0 15.9 %collective-permute-start = (bf16[160,512]{1,0:T(8,128)(2,1)S(1)}, bf16[160,512]{1,0:T(8,128)(2,1)S(1)}, u32[]{:S(2)}, u32[]{:S(2)}) collective-permute-start(bf16[160,512]{1,0:T(8,128)(2,1)S(1)} %stack_rows.2), channel_id=1, source_target_pairs={{0,24},{4,28},{8,0},{12,4},{16,8},{20,12},{24,16},{28,20},{1,25},{... | collective-permute-start | bytes 491528 | tf_op jit(solution)/shard_map/ppermute | solution.py:55
  38.6 33.4 %all-to-all-start = ((bf16[32,16,256]{2,1,0:T(8,128)(2,1)}), bf16[32,16,256]{2,1,0:T(8,128)(2,1)}, u32[]{:S(2)}, u32[]{:S(2)}) async-start(bf16[32,16,256]{2,1,0:T(8,128)(2,1)} %broadcast_in_dim.339), calls=%async_computation | async-start | bytes 524288 | tf_op jit(solution)/shard_map/all_to_all | solution.py:188
  41.9 76.2 %all-gather.3.cloned.1.call-start = ((), (), s32[]{:S(2)}) async-start(), calls=%async_computation.6 | async-start | bytes 5406720 | tf_op jit(solution)/shard_map/all_gather | solution.py:780
  42.3 20.6 %collective-permute-start.7 = (bf16[4,2,80,512]{3,2,1,0:T(8,128)(2,1)S(1)}, bf16[4,2,80,512]{3,2,1,0:T(8,128)(2,1)}, u32[]{:S(2)}, u32[]{:S(2)}) collective-permute-start(bf16[4,2,80,512]{3,2,1,0:T(8,128)(2,1)S(1)} %broadcast_select_fusion.3), channel_id=1, source_target_pairs={{0,4},{4,0},{8,12},{12,8},{16,20},{20,16},{24,28},{28,24},{1,5},{5... | collective-permute-start | bytes 1966088 | tf_op jit(solution)/shard_map/ppermute | solution.py:49
  43.9 20.4 %collective-permute-start.5 = (bf16[4,2,80,512]{3,2,1,0:T(8,128)(2,1)S(1)}, bf16[4,2,80,512]{3,2,1,0:T(8,128)(2,1)}, u32[]{:S(2)}, u32[]{:S(2)}) collective-permute-start(bf16[4,2,80,512]{3,2,1,0:T(8,128)(2,1)S(1)} %broadcast_select_fusion.2), channel_id=1, source_target_pairs={{0,2},{1,3},{2,0},{3,1},{4,6},{5,7},{6,4},{7,5},{8,10},{9,11},{10,... | collective-permute-start | bytes 1966088 | tf_op jit(solution)/shard_map/ppermute | solution.py:49
  64.2 15.7 %collective-permute-start.8 = (bf16[4,2,2,80,512]{4,3,2,1,0:T(8,128)(2,1)S(1)}, bf16[4,2,2,80,512]{4,3,2,1,0:T(8,128)(2,1)}, u32[]{:S(2)}, u32[]{:S(2)}) collective-permute-start(bf16[4,2,2,80,512]{4,3,2,1,0:T(8,128)(2,1)S(1)} %broadcast_select_fusion), channel_id=1, source_target_pairs={{0,1},{1,0},{2,3},{3,2},{4,5},{5,4},{6,7},{7,6},{8,9},{9,8},{10,11... | collective-permute-start | bytes 3932168 | tf_op jit(solution)/shard_map/ppermute | solution.py:49
  65.8 11.1 %collective-permute-start.6 = (bf16[4,2,2,80,512]{4,3,2,1,0:T(8,128)(2,1)S(1)}, bf16[4,2,2,80,512]{4,3,2,1,0:T(8,128)(2,1)}, u32[]{:S(2)}, u32[]{:S(2)}) collective-permute-start(bf16[4,2,2,80,512]{4,3,2,1,0:T(8,128)(2,1)S(1)} %broadcast_select_fusion.1), channel_id=1, source_target_pairs={{0,1},{1,0},{2,3},{3,2},{4,5},{5,4},{6,7},{7,6},{8,9},{9,8},{10,11... | collective-permute-start | bytes 3932168 | tf_op jit(solution)/shard_map/ppermute | solution.py:49
  90.2 12.7 %all-to-all-start.1 = ((bf16[32,8,128]{2,1,0:T(8,128)(2,1)}), bf16[32,8,128]{2,1,0:T(8,128)(2,1)S(1)}, u32[]{:S(2)}, u32[]{:S(2)}) async-start(bf16[32,8,128]{2,1,0:T(8,128)(2,1)} %reshape.954), calls=%async_computation.1 | async-start | bytes 131072 | tf_op jit(solution)/shard_map/all_to_all | solution.py:188
  149.9 17.0 %collective-permute-start.13 = (bf16[8,512]{1,0:T(8,128)(2,1)S(1)}, bf16[8,512]{1,0:T(8,128)(2,1)S(1)}, u32[]{:S(2)}, u32[]{:S(2)}) collective-permute-start(bf16[8,512]{1,0:T(8,128)(2,1)S(1)} %get-tuple-element.356), channel_id=1, source_target_pairs={{0,1},{1,2},{2,3},{3,4},{4,5},{5,6},{6,7},{7,8},{8,9},{9,10},{10,1... | collective-permute-start | bytes 24584 | tf_op jit(solution)/shard_map/ppermute | solution.py:195
  182.7 17.6 %all-to-all-start.3 = ((bf16[32,8,128]{2,1,0:T(8,128)(2,1)}), bf16[32,8,128]{2,1,0:T(8,128)(2,1)S(1)}, u32[]{:S(2)}, u32[]{:S(2)}) async-start(bf16[32,8,128]{2,1,0:T(8,128)(2,1)} %reshape.966), calls=%async_computation.3 | async-start | bytes 131072 | tf_op jit(solution)/shard_map/all_to_all | solution.py:188
  197.0 20.9 %collective-permute-start.15 = (bf16[2,2,2,16,2048]{4,3,0,2,1:T(8,128)(2,1)}, bf16[2,2,2,16,2048]{4,3,0,2,1:T(8,128)(2,1)}, u32[]{:S(2)}, u32[]{:S(2)}) collective-permute-start(bf16[2,2,2,16,2048]{4,3,0,2,1:T(8,128)(2,1)} %copy.105), channel_id=1, source_target_pairs={{0,2},{1,3},{2,0},{3,1},{4,6},{5,7},{6,4},{7,5},{8,10},{9,11},{10,... | collective-permute-start | bytes 1572872 | tf_op jit(solution)/shard_map/ppermute | solution.py:49
  198.8 19.2 %collective-permute-start.16 = (bf16[2,2,2,64,512]{4,3,2,1,0:T(8,128)(2,1)}, bf16[2,2,2,64,512]{4,3,2,1,0:T(8,128)(2,1)}, u32[]{:S(2)}, u32[]{:S(2)}) collective-permute-start(bf16[2,2,2,64,512]{4,3,2,1,0:T(8,128)(2,1)} %fusion.37), channel_id=1, source_target_pairs={{0,4},{4,0},{8,12},{12,8},{16,20},{20,16},{24,28},{28,24},{1,5},{5... | collective-permute-start | bytes 1572872 | tf_op jit(solution)/shard_map/ppermute | solution.py:49
  205.2 12.5 %all-to-all-start.4 = ((bf16[32,8,128]{2,1,0:T(8,128)(2,1)}), bf16[32,8,128]{2,1,0:T(8,128)(2,1)S(1)}, u32[]{:S(2)}, u32[]{:S(2)}) async-start(bf16[32,8,128]{2,1,0:T(8,128)(2,1)} %bitcast.283), calls=%async_computation.4 | async-start | bytes 131072 | tf_op jit(solution)/shard_map/all_to_all | solution.py:188
  249.7 11.3 %collective-permute-start.26 = (bf16[16,2048]{1,0:T(8,128)(2,1)S(1)}, bf16[16,2048]{1,0:T(8,128)(2,1)S(1)}, u32[]{:S(2)}, u32[]{:S(2)}) collective-permute-start(bf16[16,2048]{1,0:T(8,128)(2,1)S(1)} %fusion.90), channel_id=1, source_target_pairs={{0,16},{4,20},{8,24},{12,28},{16,0},{20,4},{24,8},{28,12},{1,17},{... | collective-permute-start | bytes 196616 | tf_op jit(solution)/shard_map/ppermute | solution.py:49
  254.9 14.1 %collective-permute-start.24 = (bf16[2,2,2,64,512]{4,3,2,1,0:T(8,128)(2,1)}, bf16[2,2,2,64,512]{4,3,2,1,0:T(8,128)(2,1)}, u32[]{:S(2)}, u32[]{:S(2)}) collective-permute-start(bf16[2,2,2,64,512]{4,3,2,1,0:T(8,128)(2,1)} %fusion.36), channel_id=1, source_target_pairs={{0,2},{1,3},{2,0},{3,1},{4,6},{5,7},{6,4},{7,5},{8,10},{9,11},{10,... | collective-permute-start | bytes 1572872 | tf_op jit(solution)/shard_map/ppermute | solution.py:49
  255.4 15.2 %collective-permute-start.25 = (bf16[2,2,2,64,512]{4,3,2,1,0:T(8,128)(2,1)}, bf16[2,2,2,64,512]{4,3,2,1,0:T(8,128)(2,1)}, u32[]{:S(2)}, u32[]{:S(2)}) collective-permute-start(bf16[2,2,2,64,512]{4,3,2,1,0:T(8,128)(2,1)} %fusion.35), channel_id=1, source_target_pairs={{0,4},{4,0},{8,12},{12,8},{16,20},{20,16},{24,28},{28,24},{1,5},{5... | collective-permute-start | bytes 1572872 | tf_op jit(solution)/shard_map/ppermute | solution.py:49
  261.0 35.1 %collective-permute-start.30 = (bf16[2,2,2,16,2048]{4,3,2,1,0:T(8,128)(2,1)}, bf16[2,2,2,16,2048]{4,3,2,1,0:T(8,128)(2,1)}, u32[]{:S(2)}, u32[]{:S(2)}) collective-permute-start(bf16[2,2,2,16,2048]{4,3,2,1,0:T(8,128)(2,1)} %fusion.34), channel_id=1, source_target_pairs={{0,4},{4,0},{8,12},{12,8},{16,20},{20,16},{24,28},{28,24},{1,5},{5... | collective-permute-start | bytes 1572872 | tf_op jit(solution)/shard_map/ppermute | solution.py:49
  264.0 68.9 %all-to-all-start.5 = ((bf16[32,16,512]{2,1,0:T(8,128)(2,1)}), bf16[32,16,512]{2,1,0:T(8,128)(2,1)}, u32[]{:S(2)}, u32[]{:S(2)}) async-start(bf16[32,16,512]{2,1,0:T(8,128)(2,1)} %bitcast.562), calls=%async_computation.5 | async-start | bytes 1048576 | tf_op jit(solution)/shard_map/all_to_all | solution.py:188
  274.3 17.3 %collective-permute-start.28 = (bf16[2,2,64,512]{3,2,1,0:T(8,128)(2,1)}, bf16[2,2,64,512]{3,2,1,0:T(8,128)(2,1)}, u32[]{:S(2)}, u32[]{:S(2)}) collective-permute-start(bf16[2,2,64,512]{3,2,1,0:T(8,128)(2,1)} %fusion.53), channel_id=1, source_target_pairs={{0,4},{4,0},{8,12},{12,8},{16,20},{20,16},{24,28},{28,24},{1,5},{5... | collective-permute-start | bytes 786440 | tf_op jit(solution)/shard_map/ppermute | solution.py:49
  274.8 16.9 %collective-permute-start.29 = (bf16[2,2,64,512]{3,2,1,0:T(8,128)(2,1)}, bf16[2,2,64,512]{3,2,1,0:T(8,128)(2,1)}, u32[]{:S(2)}, u32[]{:S(2)}) collective-permute-start(bf16[2,2,64,512]{3,2,1,0:T(8,128)(2,1)} %fusion.52), channel_id=1, source_target_pairs={{0,2},{1,3},{2,0},{3,1},{4,6},{5,7},{6,4},{7,5},{8,10},{9,11},{10,... | collective-permute-start | bytes 786440 | tf_op jit(solution)/shard_map/ppermute | solution.py:49
  299.0 22.5 %collective-permute-start.31 = (bf16[2,2,16,2048]{3,2,1,0:T(8,128)(2,1)S(1)}, bf16[2,2,16,2048]{3,2,1,0:T(8,128)(2,1)S(1)}, u32[]{:S(2)}, u32[]{:S(2)}) collective-permute-start(bf16[2,2,16,2048]{3,2,1,0:T(8,128)(2,1)S(1)} %fusion.51), channel_id=1, source_target_pairs={{0,2},{1,3},{2,0},{3,1},{4,6},{5,7},{6,4},{7,5},{8,10},{9,11},{10,... | collective-permute-start | bytes 786440 | tf_op jit(solution)/shard_map/ppermute | solution.py:49
  300.5 12.7 %collective-permute-start.37 = (bf16[128,512]{1,0:T(8,128)(2,1)}, bf16[128,512]{1,0:T(8,128)(2,1)S(1)}, u32[]{:S(2)}, u32[]{:S(2)}) collective-permute-start(bf16[128,512]{1,0:T(8,128)(2,1)} %pad_maximum_fusion.9), channel_id=1, source_target_pairs={{0,24},{4,28},{8,0},{12,4},{16,8},{20,12},{24,16},{28,20},{1,25},{... | collective-permute-start | bytes 393224 | tf_op jit(solution)/shard_map/ppermute | solution.py:55
  (204 other events, 1215.3 us)
Sparse Core Ops, SparseCore 0:
  46.2 67.9 all-gather.2
